TPU v7x, 256 devices: a whole 4x4x8 slice. The times are simulated.
256 devices in a mesh: ch: 4 (over z_hi, core), ha: 16 (over z_lo, x), dp: 4 (over y).
Axes of the slice: x: 4, y: 4, z: 8 (z_hi: 2, z_lo: 4; z = z_hi * 4 + z_lo), core: 2. Of those that a mesh axis runs over, the one named last changes fastest.
Arguments:
- features: bfloat16 [384, 4, 4, 32, 128], P('ch', 'dp', None, 'ha'), may hold values from -26 to 26
- frame_count: int32 [4], P('dp'), may hold values from 1 to 4, as said below
- norm1_gain: float32 [384], P('ch'), may hold values from 0.5 to 2
- norm1_shift: float32 [384], P('ch'), may hold values from -3 to 3
- qkv_weight: bfloat16 [384, 1152], replicated, may hold values from -0.51031036 to 0.51031036
- qkv_bias: float32 [1152], replicated, may hold values from -3 to 3
- out_weight: bfloat16 [384, 384], replicated, may hold values from -0.3125 to 0.3125
- out_bias: float32 [384], replicated, may hold values from -3 to 3
- norm2_gain: float32 [384], P('ch'), may hold values from 0.5 to 2
- norm2_shift: float32 [384], P('ch'), may hold values from -3 to 3
- conv_weight: bfloat16 [3, 3, 3, 384, 384], P(None, None, None, 'ch'), may hold values from -0.0625 to 0.0625
- conv_bias: float32 [384], P('ch'), may hold values from -3 to 3
- cotangent: bfloat16 [384, 4, 4, 32, 128], P('ch', 'dp', None, 'ha'), may hold values from -0.0234375 to 0.0234375
Outputs:
- mixed: bfloat16 [384, 4, 4, 32, 128], P('ch', 'dp', None, 'ha')
- weight_grad: float32 [3, 3, 3, 384, 384], P(None, None, None, 'ch')
Inputs may be any that keep to these rules, and one draw needn't show every extreme that they name: `frame_count`: some clip has all 4 frames valid and some clip only one.
All inputs are finite; a program needn't handle non-finite values.
Results may differ from a plain program's by a relative error of at most 0.015.
Values may be sent and summed in bfloat16 or wider, within the bound.
No kernel may reach another device: no remote copies, remote signals or barrier semaphores. Data moves between devices by JAX's collectives and lax.ppermute only.
A program may use at most 64 MiB of HBM per device.

v0:
```python
import itertools
import jax
import jax.numpy as jnp
from jax import lax
from jax.experimental import pallas as pl
from jax.experimental.pallas import tpu as pltpu
from jax.sharding import Mesh, PartitionSpec as P

EPS = 1e-06
SIZES = {"zh": 2, "co": 2, "zl": 4, "x": 4, "y": 4}
BF, F32 = jnp.bfloat16, jnp.float32
VMEM = 56 * 1024 * 1024


def permute(value, axes, target):
    sizes = [SIZES[a] for a in axes]

    def flat(index):
        at = 0
        for i, n in zip(index, sizes):
            at = at * n + i
        return at

    pairs = []
    for index in itertools.product(*[range(n) for n in sizes]):
        to = target(*index)
        if to is not None:
            pairs.append((flat(index), flat(to)))
    return lax.ppermute(value, axes, pairs)


def ring(value, axis):
    return [value] + [permute(value, (axis,), lambda i: ((i + s) % 4,)) for s in (1, 2, 3)]


def halo(last, first):
    def up(zl, x):
        at = zl * 4 + x + 1
        return (at // 4, at % 4) if at < 16 else None

    def down(zl, x):
        at = zl * 4 + x - 1
        return (at // 4, at % 4) if at >= 0 else None

    return permute(last, ("zl", "x"), up), permute(first, ("zl", "x"), down)


def spread(value, axes, count):
    copies = jnp.broadcast_to(value[None], (count,) + value.shape)
    return lax.all_to_all(copies, axes, 0, 0, tiled=True)


def cost(flops, size):
    return pl.CostEstimate(flops=flops, bytes_accessed=size, transcendentals=0)


def column(rows, place):
    lane = lax.broadcasted_iota(jnp.int32, (96, 128), 1)
    return jnp.sum(jnp.where(lane == place, rows, 0.0), axis=1, keepdims=True)


def pack_kernel(valid, frames, gain, shift, out):
    first = jnp.zeros((96, 128), F32)
    second = jnp.zeros((96, 128), F32)
    for f in range(4):
        data = frames[:, f * 256 : f * 256 + 256]
        out[2 * f, :96] = data
        out[2 * f + 1, :96] = data
        data = jnp.where(f < valid[0], data.astype(F32), 0.0)
        square = data * data
        first += data[:, :128] + data[:, 128:]
        second += square[:, :128] + square[:, 128:]
    row = lax.broadcasted_iota(jnp.int32, (96, 128), 0) // 12
    lane = lax.broadcasted_iota(jnp.int32, (96, 128), 1)
    first = jnp.sum(first, axis=1, keepdims=True)
    second = jnp.sum(second, axis=1, keepdims=True)
    sums = jnp.where(row + 96 == lane, first, jnp.where(row + 104 == lane, second, 0.0))
    sums = jnp.sum(sums, axis=0, keepdims=True)
    left = jnp.concatenate([gain[...], jnp.zeros((1, 32), F32)], axis=1) + sums
    right = jnp.concatenate([shift[...], jnp.zeros((1, 32), F32)], axis=1)
    rest = jnp.concatenate([left, right], axis=1)
    rows = []
    for _ in range(3):
        rounded = rest.astype(BF).astype(F32)
        rows.append(rounded)
        rest = rest - rounded
    rows = jnp.concatenate(rows + [jnp.zeros((13, 256), F32)], axis=0).astype(BF)
    for z in range(8):
        out[z, 96:] = rows


def attend_kernel(
    at,
    own0,
    own1,
    own2,
    own3,
    other0,
    other1,
    other2,
    other3,
    qkv,
    qkv_bias,
    out_weight,
    out_bias,
    piece0,
    piece1,
    piece2,
    piece3,
    tokens,
    scores,
    hidden,
):
    co, slot, valid, frame = at[0], at[1], at[2], at[3]
    count = valid.astype(F32) * (12 * 32 * 128)
    group = lax.broadcasted_iota(jnp.int32, (96, 128), 0) // 12
    entry = lax.broadcasted_iota(jnp.int32, (96, 128), 0)
    for which, parts in ((co, (own0, own1, own2, own3)), (1 - co, (other0, other1, other2, other3))):
        for zh in range(2):
            tables = []
            for s in range(4):
                for zl in range(4):
                    rows = parts[s][zh * 4 + zl, 96:].astype(F32)
                    tables.append(rows[0:1] + rows[1:2] + rows[2:3])
            table = tables[0]
            for other in tables[1:]:
                table = table + other
            left, right = tables[0][:, :128], tables[0][:, 128:]
            mean = column(table[:, :128], group + 96) / count
            var = column(table[:, :128], group + 104) / count - mean * mean
            scale = lax.rsqrt(var + EPS)
            gain = column(left, entry)
            shift = column(right, entry)
            rows = pl.ds(pl.multiple_of((2 * zh + which) * 96, 32), 96)
            for s in range(4):
                for zl in range(4):
                    data = parts[s][zh * 4 + zl, :96].astype(F32)
                    data = (data - mean) * scale * gain + shift
                    to = s * 1024 + zl * 256
                    tokens[rows, to : to + 256] = data.astype(BF)
    lanes = pl.ds(pl.multiple_of(slot * 256, 256), 256)
    queries = lax.dot_general(
        tokens[:, lanes], qkv[:, :384], (((0,), (0,)), ((), ())), preferred_element_type=F32
    )
    queries = (queries + qkv_bias[:, :384]).astype(BF)
    lifted = lax.dot_general(
        queries, qkv[:, 384:768], (((1,), (1,)), ((), ())), preferred_element_type=F32
    ).astype(BF)
    offset = jnp.sum(queries.astype(F32) * qkv_bias[:, 384:768], axis=1, keepdims=True)
    top = jnp.full((256, 128), -jnp.inf, F32)
    for j in range(8):
        piece = jnp.dot(lifted, tokens[:, j * 512 : j * 512 + 512], preferred_element_type=F32)
        piece = (piece + offset) * (384 ** (-0.5))
        scores[:, j * 512 : j * 512 + 512] = piece
        for i in range(4):
            top = jnp.maximum(top, piece[:, i * 128 : i * 128 + 128])
    top = jnp.max(top, axis=1, keepdims=True)
    total = jnp.zeros((256, 128), F32)
    acc = jnp.zeros((256, 384), F32)
    for j in range(8):
        ew = jnp.exp(scores[:, j * 512 : j * 512 + 512] - top)
        for i in range(4):
            total += ew[:, i * 128 : i * 128 + 128]
        acc += lax.dot_general(
            ew.astype(BF),
            tokens[:, j * 512 : j * 512 + 512],
            (((1,), (1,)), ((), ())),
            preferred_element_type=F32,
        )
    total = jnp.sum(total, axis=1, keepdims=True)
    acc = (acc / total).astype(BF)
    attended = jnp.dot(acc, qkv[:, 768:], preferred_element_type=F32)
    attended = (attended + qkv_bias[:, 768:]).astype(BF)
    update = lax.dot_general(
        out_weight[...], attended, (((0,), (1,)), ((), ())), preferred_element_type=F32
    )
    hidden[...] = (update + out_bias[...]).astype(BF)
    for which, part in ((co, own0), (1 - co, other0)):
        for zh in range(2):
            rows = pl.ds(pl.multiple_of((2 * zh + which) * 96, 32), 96)
            raw = part[zh * 4 + slot, :96].astype(F32)
            hidden[rows, :] = (raw + hidden[rows, :].astype(F32)).astype(BF)
    for k, piece in enumerate((piece0, piece1, piece2, piece3)):
        piece[...] = hidden[pl.ds(pl.multiple_of((frame ^ k) * 96, 32), 96), :]


def arrange_kernel(at, piece0, piece1, piece2, piece3, whole, last, leading, sums, held):
    for k, piece in enumerate((piece0, piece1, piece2, piece3)):
        held[at[0] ^ k] = piece[...]
    valid = at[1]
    first = jnp.zeros((96, 128), F32)
    second = jnp.zeros((96, 128), F32)
    for f in range(4):
        data = held[f]
        whole[:, f * 256 : f * 256 + 256] = data
        leading[:, f * 128 : f * 128 + 128] = data[:, :128]
        last[:, f * 128 : f * 128 + 128] = data[:, 128:]
        data = jnp.where(f < valid, data.astype(F32), 0.0)
        square = data * data
        first += data[:, :128] + data[:, 128:]
        second += square[:, :128] + square[:, 128:]
    first = jnp.sum(first, axis=1, keepdims=True)
    second = jnp.sum(second, axis=1, keepdims=True)
    row = lax.broadcasted_iota(jnp.int32, (96, 128), 0) // 12
    lane = lax.broadcasted_iota(jnp.int32, (96, 128), 1)
    table = jnp.where(row == lane, first, jnp.where(row + 8 == lane, second, 0.0))
    table = jnp.sum(table, axis=0, keepdims=True)
    table = table + jnp.where(lane[0:1] == 64, valid.astype(F32) / 16.0, 0.0)
    sums[...] = jnp.broadcast_to(table[None], sums.shape)


def clip_columns(table):
    group = lax.broadcasted_iota(jnp.int32, (96, 128), 0) // 12
    count = column(table, 64) * (12 * 32 * 128)
    mean = column(table, group) / count
    var = column(table, group + 8) / count - mean * mean
    return mean, lax.rsqrt(var + EPS)


def gate(data, columns, gain, shift):
    mean, scale = columns
    u = (data.astype(F32) - mean) * scale * gain[...] + shift[...]
    return u / (1.0 + jnp.exp(-u))


def shifted(g, kx):
    if kx == 1:
        return g
    lane = lax.broadcasted_iota(jnp.int32, g.shape, 1)
    if kx == 0:
        return jnp.where(lane == 0, 0.0, pltpu.roll(g, 1, 1))
    return jnp.where(lane == 127, 0.0, pltpu.roll(g, 127, 1))


def grad_kernel(
    at,
    table,
    clip0,
    clip1,
    clip2,
    clip3,
    near0,
    near1,
    far0,
    far1,
    gain,
    shift,
    out,
    gs,
    cs,
    cot,
    before,
    after,
):
    for i, part in enumerate((near0, near1, far0, far1)):
        cot[i] = part[:, :1024]
        before[i] = part[:, 1024:1536]
        after[i] = part[:, 1536:]
    gs[864:, :] = jnp.zeros((32, 4096), BF)
    for s, hidden in enumerate((clip0, clip1, clip2, clip3)):
        clip = lax.rem(at[0] - s + 4, 4)
        columns = clip_columns(jnp.sum(table[:, clip], axis=0))
        for kt in range(2):
            gs[kt * 288 : kt * 288 + 288, s * 1024 : s * 1024 + (2 - kt) * 256] = jnp.zeros(
                (288, (2 - kt) * 256), BF
            )
        for b in range(8):
            g = gate(hidden[:, b * 128 : b * 128 + 128], columns, gain, shift)
            for kx in range(3):
                piece = shifted(g, kx).astype(BF)
                for kt in range(3):
                    to = b * 128 + (2 - kt) * 256
                    if to < 1024:
                        row = (kt * 3 + kx) * 96
                        gs[row : row + 96, s * 1024 + to : s * 1024 + to + 128] = piece
        k = jnp.where(lax.rem(clip, 2) == at[1], 0, 2) + (clip // 2 ^ at[2])
        cs[96:192, s * 1024 : s * 1024 + 1024] = cot[k]
        for f in range(4):
            to = s * 1024 + f * 256
            cs[0:96, to : to + 128] = cot[k, :, f * 256 + 128 : f * 256 + 256]
            cs[0:96, to + 128 : to + 256] = after[k, :, f * 128 : f * 128 + 128]
            cs[192:288, to : to + 128] = before[k, :, f * 128 : f * 128 + 128]
            cs[192:288, to + 128 : to + 256] = cot[k, :, f * 256 : f * 256 + 128]
    grads = lax.dot_general(
        cs[...], gs[...], (((1,), (1,)), ((), ())), preferred_element_type=F32
    ).astype(BF)
    for t in range(18):
        for l in range(7):
            out[t * 7 + l] = grads[t * 16 : t * 16 + 16, l * 128 : l * 128 + 128]
    out[126:] = jnp.zeros((2, 16, 128), BF)


def join_kernel(at, table0, table1, table2, table3, out, held):
    for s, table in enumerate((table0, table1, table2, table3)):
        held[lax.rem(at[0] - s + 4, 4)] = table[...]
    for ky in range(3):
        for l in range(7):
            blocks = [
                held[j, (ky * 6 + t) * 7 + l] for j in range(4) for t in range(6)
            ]
            flipped = jnp.concatenate(blocks, axis=0).astype(F32).T
            lane = l * 128
            while lane < min(l * 128 + 128, 864):
                block = lane // 96
                end = min((block + 1) * 96, l * 128 + 128)
                row = ((block // 3 * 3 + ky) * 3 + block % 3) * 96 + lane % 96
                out[row : row + end - lane, :] = flipped[lane - l * 128 : end - l * 128, :]
                lane = end


def conv_kernel(at, table, clip, before, after, weight, gain, shift, keep, send, stack, held):
    stack[:, :512] = jnp.zeros((864, 512), BF)
    columns = clip_columns(jnp.sum(table[:, at[2]], axis=0))
    for f in range(4):
        for p in range(4):
            if p == 0:
                g = before[:, f * 128 : f * 128 + 128]
            elif p == 3:
                g = after[:, f * 128 : f * 128 + 128]
            else:
                g = clip[:, f * 256 + p * 128 - 128 : f * 256 + p * 128]
            g = gate(g, columns, gain, shift)
            if p == 0:
                g = jnp.where(at[1] > 0, g, 0.0)
            elif p == 3:
                g = jnp.where(at[1] < 15, g, 0.0)
            for kx in range(3):
                piece = shifted(g, kx).astype(BF)
                for ky in range(3):
                    r = p - ky
                    if 0 <= r < 2:
                        to = 512 + f * 256 + r * 128
                        row = (ky * 3 + kx) * 96
                        stack[row : row + 96, to : to + 128] = piece
    total = jnp.zeros((384, 1024), F32)
    for kt in range(3):
        total = total + jnp.dot(
            weight[kt], stack[:, kt * 256 : kt * 256 + 1024], preferred_element_type=F32
        )
    held[...] = total.astype(BF).reshape(4, 96, 1024)
    for zh in range(2):
        keep[zh] = held[2 * zh + at[0]]
        send[zh] = held[2 * zh + 1 - at[0]]


def body(
    features,
    frame_count,
    norm1_gain,
    norm1_shift,
    qkv_weight,
    qkv_bias,
    out_weight,
    out_bias,
    norm2_gain,
    norm2_shift,
    conv_weight,
    conv_bias,
    cotangent,
):
    zh, co, zl = lax.axis_index("zh"), lax.axis_index("co"), lax.axis_index("zl")
    x, y = lax.axis_index("x"), lax.axis_index("y")
    ch = zh * 2 + co
    params = pltpu.CompilerParams(vmem_limit_bytes=VMEM)
    scalars = pl.BlockSpec(memory_space=pltpu.SMEM)
    whole = pl.BlockSpec(memory_space=pltpu.VMEM)
    valid = frame_count[0]
    mask = (lax.iota(jnp.int32, 4) < valid).astype(F32)

    by_frame = pl.pallas_call(
        pack_kernel,
        out_shape=jax.ShapeDtypeStruct((8, 112, 256), BF),
        in_specs=[scalars, whole, whole, whole],
        out_specs=whole,
        compiler_params=params,
        cost_estimate=cost(10**6, 200000),
        name="pack",
    )(frame_count, features.reshape(96, 1024), norm1_gain[None], norm1_shift[None])
    mine = lax.all_to_all(by_frame, ("zh", "zl"), 0, 0, tiled=True)
    masked = (cotangent.reshape(96, 4, 256) * mask.astype(BF)[None, :, None]).reshape(96, 1024)
    lines = masked.reshape(96, 4, 2, 128)
    before, after = halo(lines[:, :, 1].reshape(96, 512), lines[:, :, 0].reshape(96, 512))
    bundle = jnp.concatenate([masked, before, after], axis=1)
    mine, bundle = lax.optimization_barrier((mine, bundle))
    parts = ring(mine, "x")

    near = [
        permute(
            bundle, ("zh", "co", "y"), lambda zh, co, y: ((y // 2 + k) % 2, y % 2, 2 * zh + co)
        )
        for k in range(2)
    ]

    parts[2], near = lax.optimization_barrier((parts[2], near))
    others = [permute(p, ("co",), lambda i: (1 - i,)) for p in parts]

    frame = 2 * zh + zl // 2
    at = jnp.stack([co, 2 * (zl % 2) + co, valid, frame]).astype(jnp.int32)
    pieces = pl.pallas_call(
        attend_kernel,
        out_shape=[jax.ShapeDtypeStruct((96, 256), BF)] * 4,
        in_specs=[scalars] + [whole] * 12,
        out_specs=[whole] * 4,
        scratch_shapes=[
            pltpu.VMEM((384, 4096), BF),
            pltpu.VMEM((256, 4096), F32),
            pltpu.VMEM((384, 256), BF),
        ],
        compiler_params=params,
        cost_estimate=cost(4 * 10**9, 20 * 10**6),
        name="attention",
    )(
        at,
        *parts,
        *others,
        qkv_weight,
        qkv_bias[None],
        out_weight,
        out_bias[:, None],
    )

    pieces = list(pieces)

    for k in range(4):

        def to_channels(zh, co, zl, k=k):
            c = (2 * zh + zl // 2) ^ k
            return (c // 2, c % 2, 2 * (zl % 2) + co)

        pieces[k] = permute(pieces[k], ("zh", "co", "zl"), to_channels)
    hidden, last, leading, packed = pl.pallas_call(
        arrange_kernel,
        out_shape=(
            jax.ShapeDtypeStruct((96, 1024), BF),
            jax.ShapeDtypeStruct((96, 512), BF),
            jax.ShapeDtypeStruct((96, 512), BF),
            jax.ShapeDtypeStruct((64, 1, 128), F32),
        ),
        in_specs=[scalars] + [whole] * 4,
        out_specs=(whole,) * 4,
        scratch_shapes=[pltpu.VMEM((4, 96, 256), BF)],
        compiler_params=params,
        cost_estimate=cost(10**6, 10**6),
        name="arrange",
    )(jnp.stack([ch, valid]).astype(jnp.int32), *pieces)
    clips = ring(hidden, "y")
    near, _ = lax.optimization_barrier((near, hidden))
    far = [permute(v, ("co",), lambda i: (1 - i,)) for v in near]

    packed = lax.all_to_all(packed, ("zl", "x", "y"), 0, 0, tiled=True)
    packed = packed.reshape(16, 4, 1, 128)
    gain, shift = norm2_gain[:, None], norm2_shift[:, None]

    table = pl.pallas_call(
        grad_kernel,
        out_shape=jax.ShapeDtypeStruct((128, 16, 128), BF),
        in_specs=[scalars] + [whole] * 11,
        out_specs=whole,
        scratch_shapes=[
            pltpu.VMEM((896, 4096), BF),
            pltpu.VMEM((288, 4096), BF),
            pltpu.VMEM((4, 96, 1024), BF),
            pltpu.VMEM((4, 96, 512), BF),
            pltpu.VMEM((4, 96, 512), BF),
        ],
        compiler_params=params,
        cost_estimate=cost(4 * 10**9, 20 * 10**6),
        name="weight_grad",
    )(jnp.stack([y, co, zh]).astype(jnp.int32), packed, *clips, *near, *far, gain, shift)
    table, conv_weight, last, leading = lax.optimization_barrier((table, conv_weight, last, leading))
    above, below = halo(last, leading)
    kernels = conv_weight.transpose(0, 4, 1, 2, 3).reshape(3, 384, 864)
    shares = lax.all_to_all(table.reshape(16, 8, 16, 128), ("zl", "x"), 0, 0, tiled=True)
    keep, send = pl.pallas_call(
        conv_kernel,
        out_shape=(jax.ShapeDtypeStruct((2, 96, 1024), BF),) * 2,
        in_specs=[scalars] + [whole] * 7,
        out_specs=(whole, whole),
        scratch_shapes=[pltpu.VMEM((864, 1536), BF), pltpu.VMEM((4, 96, 1024), BF)],
        compiler_params=params,
        cost_estimate=cost(3 * 10**9, 12 * 10**6),
        name="convolution",
    )(
        jnp.stack([co, zl * 4 + x, y]).astype(jnp.int32),
        packed,
        clips[0],
        above,
        below,
        kernels,
        gain,
        shift,
    )
    send = permute(send, ("co",), lambda i: (1 - i,))
    summed = keep.astype(F32) + send.astype(F32)
    near = lax.dynamic_index_in_dim(summed, zh, 0, keepdims=False)
    far = lax.dynamic_index_in_dim(summed, 1 - zh, 0, keepdims=False).astype(BF)
    shares, near, far = lax.optimization_barrier((shares, near, far))
    share = jnp.sum(shares.astype(F32), axis=0).astype(BF)
    table = spread(share, ("zl", "x"), 16).reshape(128, 16, 128)
    table, near, far = lax.optimization_barrier((table, near, far))
    weight_grad = pl.pallas_call(
        join_kernel,
        out_shape=jax.ShapeDtypeStruct((2592, 384), F32),
        in_specs=[scalars] + [whole] * 4,
        out_specs=whole,
        scratch_shapes=[pltpu.VMEM((4, 128, 16, 128), BF)],
        compiler_params=params,
        cost_estimate=cost(10**6, 6 * 10**6),
        name="join",
    )(y.astype(jnp.int32)[None], *ring(table, "y"))
    weight_grad = weight_grad.reshape(3, 3, 3, 96, 384)

    conv = near + permute(far, ("zh",), lambda i: (1 - i,)).astype(F32)
    mixed = hidden.astype(F32) + conv + conv_bias[:, None]
    mixed = (mixed.reshape(96, 4, 256) * mask[None, :, None]).astype(BF)
    return mixed.reshape(96, 1, 4, 2, 128), weight_grad


def solution(mesh):
    cut = Mesh(mesh.devices.reshape(2, 2, 4, 4, 4), ("zh", "co", "zl", "x", "y"))
    ch, ha = ("zh", "co"), ("zl", "x")
    maps = P(ch, "y", None, ha, None)
    placed = (
        maps,
        P("y"),
        P(ch),
        P(ch),
        P(),
        P(),
        P(),
        P(),
        P(ch),
        P(ch),
        P(None, None, None, ch, None),
        P(ch),
        maps,
    )
    return jax.shard_map(
        body,
        mesh=cut,
        in_specs=placed,
        out_specs=(maps, P(None, None, None, ch, None)),
        check_vma=False,
    )
```

profile of v0, /device:TPU:65, one launch (start us, length us, event | category | flops | bytes accessed | tf_op | source)
XLA Modules:
  0.0 203.7 jit_solution(3412946759809737530)
XLA Ops:
  1.3 1.7 reshape.59.frames
  3.0 1.9 pack.1
  4.9 7.7 %all-to-all-start = ((bf16[8,112,256]{2,1,0:T(8,128)(2,1)}), bf16[8,112,256]{2,1,0:T(8,128)(2,1)S(1)}, u32[]{:S(2)}, u32[]{:S(2)}) async-start(bf16[8,112,256]{2,1,0:T(8,128)(2,1)} %pack.1), calls=%async_computation | async-start | bytes 917504 | tf_op jit(solution)/shard_map/all_to_all | solution.py:379
  12.9 1.1 slice_reduce_fusion.1
  14.0 4.4 %collective-permute-start.1 = (bf16[96,512]{1,0:T(8,128)(2,1)S(1)}, bf16[96,512]{1,0:T(8,128)(2,1)S(1)}, u32[]{:S(2)}, u32[]{:S(2)}) collective-permute-start(bf16[96,512]{1,0:T(8,128)(2,1)S(1)} %bitcast.51), channel_id=1, source_target_pairs={{4,0},{8,4},{12,8},{16,12},{20,16},{24,20},{28,24},{32,28},{36,32}... | collective-permute-start | bytes 294920 | tf_op jit(solution)/shard_map/ppermute | solution.py:29
  18.4 1.9 collective-permute-start
  20.6 2.2 %collective-permute-done.1 = bf16[96,512]{1,0:T(8,128)(2,1)S(1)} collective-permute-done((bf16[96,512]{1,0:T(8,128)(2,1)S(1)}, bf16[96,512]{1,0:T(8,128)(2,1)S(1)}, u32[]{:S(2)}, u32[]{:S(2)}) %collective-permute-start.1) | collective-permute-done | bytes 98336 | tf_op jit(solution)/shard_map/ppermute | solution.py:29
  22.8 3.6 %collective-permute-done = bf16[96,512]{1,0:T(8,128)(2,1)S(1)} collective-permute-done((bf16[96,512]{1,0:T(8,128)(2,1)S(1)}, bf16[96,512]{1,0:T(8,128)(2,1)S(1)}, u32[]{:S(2)}, u32[]{:S(2)}) %collective-permute-start) | collective-permute-done | bytes 98336 | tf_op jit(solution)/shard_map/ppermute | solution.py:29
  26.5 0.7 collective-permute-start.3
  27.2 1.3 collective-permute-start.6
  28.5 0.5 collective-permute-start.2
  29.0 8.0 %collective-permute-start.5 = (bf16[96,2048]{1,0:T(8,128)(2,1)S(1)}, bf16[96,2048]{1,0:T(8,128)(2,1)}, u32[]{:S(2)}, u32[]{:S(2)}) collective-permute-start(bf16[96,2048]{1,0:T(8,128)(2,1)S(1)} %pad_maximum_fusion), channel_id=1, source_target_pairs={{0,128},{1,192},{2,0},{3,64},{64,129},{65,193},{66,1},{67,65},{128... | collective-permute-start | bytes 1179656 | tf_op jit(solution)/shard_map/ppermute | solution.py:29
  37.0 1.9 collective-permute-start.4
  38.9 14.4 %collective-permute-done.5.near1 = bf16[96,2048]{1,0:T(8,128)(2,1)} collective-permute-done((bf16[96,2048]{1,0:T(8,128)(2,1)S(1)}, bf16[96,2048]{1,0:T(8,128)(2,1)}, u32[]{:S(2)}, u32[]{:S(2)}) %collective-permute-start.5) | collective-permute-done | bytes 393248 | tf_op jit(solution)/shard_map/ppermute | solution.py:29
  53.3 0.3 collective-permute-start.7
  54.0 0.3 collective-permute-start.10
  54.6 0.6 broadcast_in_dim.30.qkv_bias
  55.2 0.8 broadcast_in_dim.35.out_bias
  56.0 0.7 pad_add_fusion.1.at
  56.6 0.5 collective-permute-done.10.other3
  57.4 0.5 copy-done.23
  58.1 9.0 %attention.1 = (bf16[96,256]{1,0:T(8,128)(2,1)}, bf16[96,256]{1,0:T(8,128)(2,1)}, bf16[96,256]{1,0:T(8,128)(2,1)}, bf16[96,256]{1,0:T(8,128)(2,1)}) custom-call(s32[4]{0:T(128)} %pad_add_fusion.1.at, bf16[8,112,256]{2,1,0:T(8,128)(2,1)} %copy-done.6, bf16[8,112,256]{2,1,0:T(8,128)(2,1)} %copy-done.20, bf16[8,112,256]{2,1,0:T(8,128)(2,1)} %copy-done.18, ...), custom_call_target="tpu_custom_call" | custom-call | flops 4000000000 | bytes 20000000 | tf_op jit(solution)/shard_map/attention/pallas_call | solution.py:399
  67.1 2.9 %collective-permute-start.11 = (bf16[96,256]{1,0:T(8,128)(2,1)}, bf16[96,256]{1,0:T(8,128)(2,1)S(1)}, u32[]{:S(2)}, u32[]{:S(2)}) collective-permute-start(bf16[96,256]{1,0:T(8,128)(2,1)} %get-tuple-element.32), channel_id=1, source_target_pairs={{0,0},{16,32},{32,64},{48,96},{64,16},{80,48},{96,80},{112,112},{1... | collective-permute-start | bytes 147464 | tf_op jit(solution)/shard_map/ppermute | solution.py:29
  69.9 1.0 collective-permute-start.12
  71.0 8.1 %collective-permute-start.13 = (bf16[96,256]{1,0:T(8,128)(2,1)}, bf16[96,256]{1,0:T(8,128)(2,1)S(1)}, u32[]{:S(2)}, u32[]{:S(2)}) collective-permute-start(bf16[96,256]{1,0:T(8,128)(2,1)} %get-tuple-element.34), channel_id=1, source_target_pairs={{0,128},{16,160},{32,192},{48,224},{64,144},{80,176},{96,208},{112... | collective-permute-start | bytes 147464 | tf_op jit(solution)/shard_map/ppermute | solution.py:29
  79.1 2.3 %collective-permute-start.14 = (bf16[96,256]{1,0:T(8,128)(2,1)}, bf16[96,256]{1,0:T(8,128)(2,1)S(1)}, u32[]{:S(2)}, u32[]{:S(2)}) collective-permute-start(bf16[96,256]{1,0:T(8,128)(2,1)} %get-tuple-element.35), channel_id=1, source_target_pairs={{0,192},{16,224},{32,128},{48,160},{64,208},{80,240},{96,144},{112... | collective-permute-start | bytes 147464 | tf_op jit(solution)/shard_map/ppermute | solution.py:29
  81.4 0.6 pad_add_fusion.at
  82.0 1.6 collective-permute-done.13.piece2
  83.6 2.2 %collective-permute-done.14.piece3 = bf16[96,256]{1,0:T(8,128)(2,1)S(1)} collective-permute-done((bf16[96,256]{1,0:T(8,128)(2,1)}, bf16[96,256]{1,0:T(8,128)(2,1)S(1)}, u32[]{:S(2)}, u32[]{:S(2)}) %collective-permute-start.14) | collective-permute-done | bytes 49184 | tf_op jit(solution)/shard_map/ppermute | solution.py:29
  85.8 0.6 copy-done.11
  86.4 1.7 arrange.1
  88.1 1.5 collective-permute-start.18
  89.7 1.5 collective-permute-start.17
  91.2 1.2 collective-permute-start.16
  92.4 0.9 collective-permute-start.15
  93.3 0.7 copy.22.gain
  94.0 0.7 copy.23.shift
  94.7 10.4 %all-to-all-start.1 = ((f32[64,1,128]{2,1,0:T(1,128)}), f32[64,1,128]{2,1,0:T(1,128)S(1)}, u32[]{:S(2)}, u32[]{:S(2)}) async-start(f32[64,1,128]{2,1,0:T(1,128)} %get-tuple-element.37), calls=%async_computation.1 | async-start | bytes 65536 | tf_op jit(solution)/shard_map/all_to_all | solution.py:450
  105.1 0.6 pad_add_fusion.2.at
  105.7 6.5 %all-to-all-done.1 = f32[64,1,128]{2,1,0:T(1,128)S(1)} async-done(((f32[64,1,128]{2,1,0:T(1,128)}), f32[64,1,128]{2,1,0:T(1,128)S(1)}, u32[]{:S(2)}, u32[]{:S(2)}) %all-to-all-start.1) | async-done | bytes 32800 | tf_op jit(solution)/shard_map/all_to_all | solution.py:450
  112.3 0.5 copy-done.12
  113.2 6.5 %weight_grad.1 = bf16[128,16,128]{2,1,0:T(8,128)(2,1)} custom-call(s32[3]{0:T(128)} %pad_add_fusion.2.at, f32[16,4,1,128]{3,2,1,0:T(1,128)} %bitcast.53, bf16[96,1024]{1,0:T(8,128)(2,1)} %get-tuple-element.36.clip0.clip, bf16[96,1024]{1,0:T(8,128)(2,1)} %copy-done.28, bf16[96,1024]{1,0:T(8,128)(2,1)} %copy-done.27, bf16[96,1024]{1,0:T(8,128)(2,1)} %copy-done.26, ...), custom_call_target="tpu_custom_call" | custom-call | flops 4000000000 | bytes 20000000 | tf_op jit(solution)/shard_map/weight_grad/pallas_call | solution.py:454
  119.8 2.2 %collective-permute-start.20 = (bf16[96,512]{1,0:T(8,128)(2,1)}, bf16[96,512]{1,0:T(8,128)(2,1)S(1)}, u32[]{:S(2)}, u32[]{:S(2)}) collective-permute-start(bf16[96,512]{1,0:T(8,128)(2,1)} %get-tuple-element.45), channel_id=1, source_target_pairs={{0,4},{4,8},{8,12},{12,16},{16,20},{20,24},{24,28},{28,32},{32,36}... | collective-permute-start | bytes 294920 | tf_op jit(solution)/shard_map/ppermute | solution.py:29
  122.0 5.2 %collective-permute-start.21 = (bf16[96,512]{1,0:T(8,128)(2,1)}, bf16[96,512]{1,0:T(8,128)(2,1)S(1)}, u32[]{:S(2)}, u32[]{:S(2)}) collective-permute-start(bf16[96,512]{1,0:T(8,128)(2,1)} %get-tuple-element.46), channel_id=1, source_target_pairs={{4,0},{8,4},{12,8},{16,12},{20,16},{24,20},{28,24},{32,28},{36,32}... | collective-permute-start | bytes 294920 | tf_op jit(solution)/shard_map/ppermute | solution.py:29
  127.2 0.6 pad_add_fusion.3.at
  127.7 3.8 %all-to-all-start.2 = ((bf16[16,8,16,128]{3,2,1,0:T(8,128)(2,1)}), bf16[16,8,16,128]{3,2,1,0:T(8,128)(2,1)S(1)}, u32[]{:S(2)}, u32[]{:S(2)}) async-start(bf16[16,8,16,128]{3,2,1,0:T(8,128)(2,1)} %bitcast.48), calls=%async_computation.2 | async-start | bytes 1048576 | tf_op jit(solution)/shard_map/all_to_all | solution.py:473
  131.5 2.4 %copy.24.weight = bf16[3,384,864]{2,1,0:T(8,128)(2,1)} copy(bf16[3,384,864]{1,2,0:T(8,128)(2,1)S(1)} %bitcast.47) | data formatting | bytes 3981312 | tf_op jit(solution)/shard_map/reshape | solution.py:472
  133.9 0.6 copy-done.29
  134.5 0.6 copy-done.30
  135.2 5.8 %convolution.1 = (bf16[2,96,1024]{2,1,0:T(8,128)(2,1)}, bf16[2,96,1024]{2,1,0:T(8,128)(2,1)}) custom-call(s32[3]{0:T(128)} %pad_add_fusion.3.at, f32[16,4,1,128]{3,2,1,0:T(1,128)} %bitcast.54, bf16[96,1024]{1,0:T(8,128)(2,1)} %get-tuple-element.36.clip0.clip, bf16[96,512]{1,0:T(8,128)(2,1)} %copy-done.29, bf16[96,512]{1,0:T(8,128)(2,1)} %copy-done.30, ...), custom_call_target="tpu_custom_call" | custom-call | flops 3000000000 | bytes 12000000 | tf_op jit(solution)/shard_map/convolution/pallas_call | solution.py:474
  141.0 3.9 %collective-permute-start.22 = (bf16[2,96,1024]{2,1,0:T(8,128)(2,1)}, bf16[2,96,1024]{2,1,0:T(8,128)(2,1)S(1)}, u32[]{:S(2)}, u32[]{:S(2)}) collective-permute-start(bf16[2,96,1024]{2,1,0:T(8,128)(2,1)} %get-tuple-element.49), channel_id=1, source_target_pairs={{0,64},{64,0},{1,65},{65,1},{2,66},{66,2},{3,67},{67,3},{4,68},{68... | collective-permute-start | bytes 1179656 | tf_op jit(solution)/shard_map/ppermute | solution.py:29
  144.9 1.6 collective-permute-done.22
  146.4 1.1 convert_add_fusion
  147.9 21.4 %all_to_all.20 = bf16[16,8,16,128]{3,2,1,0:T(8,128)(2,1)S(1)} all-to-all(bf16[16,8,16,128]{3,2,1,0:T(8,128)(2,1)S(1)} %broadcast_in_dim.34), channel_id=1, replica_groups=mesh['zh'=2,'co'=2,'zl'=4,'x'=4,'y'=4] {'zl','x'}, dimensions={0} | all-to-all | bytes 1048576 | tf_op jit(solution)/shard_map/all_to_all | solution.py:50
  169.2 1.9 collective-permute-start.23
  171.1 0.9 collective-permute-start.26
  172.0 1.2 collective-permute-start.25
  173.1 10.3 %collective-permute-done.23 = bf16[96,1024]{1,0:T(8,128)(2,1)S(1)} collective-permute-done((bf16[96,1024]{1,0:T(8,128)(2,1)S(1)}, bf16[96,1024]{1,0:T(8,128)(2,1)S(1)}, u32[]{:S(2)}, u32[]{:S(2)}) %collective-permute-start.23) | collective-permute-done | bytes 196640 | tf_op jit(solution)/shard_map/ppermute | solution.py:29
  183.5 0.3 reshape.66
  183.8 0.9 fusion
  184.7 0.5 collective-permute-done.25.table2
  185.2 13.3 %collective-permute-done.24.table1 = bf16[128,16,128]{2,1,0:T(8,128)(2,1)S(1)} collective-permute-done((bf16[128,16,128]{2,1,0:T(8,128)(2,1)S(1)}, bf16[128,16,128]{2,1,0:T(8,128)(2,1)S(1)}, u32[]{:S(2)}, u32[]{:S(2)}) %collective-permute-start.24) | collective-permute-done | bytes 524320 | tf_op jit(solution)/shard_map/ppermute | solution.py:29
  198.6 0.8 copy-done.5
  199.4 4.4 %join.1 = f32[2592,384]{1,0:T(8,128)} custom-call(s32[1]{0:T(128)} %bitcast.8.at, bf16[128,16,128]{2,1,0:T(8,128)(2,1)} %bitcast.46, bf16[128,16,128]{2,1,0:T(8,128)(2,1)} %copy-done.5, bf16[128,16,128]{2,1,0:T(8,128)(2,1)} %copy-done.4, bf16[128,16,128]{2,1,0:T(8,128)(2,1)} %copy-done.3), custom_call_target="tpu_custom_call" | custom-call | flops 1000000 | bytes 6000000 | tf_op jit(solution)/shard_map/join/pallas_call | solution.py:501
  (94 shorter events, 2.5 us)
Async XLA Ops:
  0.6 12.0 %copy-start.2 = (bf16[96,1,4,2,128]{4,3,2,1,0:T(2,128)(2,1)S(1)}, bf16[96,1,4,2,128]{4,3,2,1,0:T(2,128)(2,1)}, u32[]{:S(2)}) copy-start(bf16[96,1,4,2,128]{4,3,2,1,0:T(2,128)(2,1)} %param.25) | copy-start | bytes 589828
  4.9 49.7 %copy-start.13 = (f32[1152]{0:T(1024)S(1)}, f32[1152]{0:T(1024)}, u32[]{:S(2)}) copy-start(f32[1152]{0:T(1024)} %param.18) | copy-start | bytes 13828
  4.9 50.2 %copy-start.14 = (f32[384]{0:T(512)S(1)}, f32[384]{0:T(512)}, u32[]{:S(2)}) copy-start(f32[384]{0:T(512)} %param.20) | copy-start | bytes 4612
  4.9 21.5 %all-to-all-start = ((bf16[8,112,256]{2,1,0:T(8,128)(2,1)}), bf16[8,112,256]{2,1,0:T(8,128)(2,1)S(1)}, u32[]{:S(2)}, u32[]{:S(2)}) async-start(bf16[8,112,256]{2,1,0:T(8,128)(2,1)} %pack.1), calls=%async_computation | async-start | bytes 917504 | tf_op jit(solution)/shard_map/all_to_all | solution.py:379
  14.0 8.8 %collective-permute-start.1 = (bf16[96,512]{1,0:T(8,128)(2,1)S(1)}, bf16[96,512]{1,0:T(8,128)(2,1)S(1)}, u32[]{:S(2)}, u32[]{:S(2)}) collective-permute-start(bf16[96,512]{1,0:T(8,128)(2,1)S(1)} %bitcast.51), channel_id=1, source_target_pairs={{4,0},{8,4},{12,8},{16,12},{20,16},{24,20},{28,24},{32,28},{36,32}... | collective-permute-start | bytes 294920 | tf_op jit(solution)/shard_map/ppermute | solution.py:29
  18.4 8.0 %collective-permute-start = (bf16[96,512]{1,0:T(8,128)(2,1)S(1)}, bf16[96,512]{1,0:T(8,128)(2,1)S(1)}, u32[]{:S(2)}, u32[]{:S(2)}) collective-permute-start(bf16[96,512]{1,0:T(8,128)(2,1)S(1)} %bitcast.52), channel_id=1, source_target_pairs={{0,4},{4,8},{8,12},{12,16},{16,20},{20,24},{24,28},{28,32},{32,36}... | collective-permute-start | bytes 294920 | tf_op jit(solution)/shard_map/ppermute | solution.py:29
  26.5 30.8 %copy-start.6 = (bf16[8,112,256]{2,1,0:T(8,128)(2,1)}, bf16[8,112,256]{2,1,0:T(8,128)(2,1)S(1)}, u32[]{:S(2)}) copy-start(bf16[8,112,256]{2,1,0:T(8,128)(2,1)S(1)} %all-to-all-done.own0) | copy-start | bytes 1376260
  26.5 27.2 %collective-permute-start.3 = (bf16[8,112,256]{2,1,0:T(8,128)(2,1)S(1)}, bf16[8,112,256]{2,1,0:T(8,128)(2,1)S(1)}, u32[]{:S(2)}, u32[]{:S(2)}) collective-permute-start(bf16[8,112,256]{2,1,0:T(8,128)(2,1)S(1)} %all-to-all-done.own0), channel_id=1, source_target_pairs={{0,8},{4,12},{8,0},{12,4},{1,9},{5,13},{9,1},{13,5},{2,10},{6,14},... | collective-permute-start | bytes 1376264 | tf_op jit(solution)/shard_map/ppermute | solution.py:29
  27.2 26.7 %collective-permute-start.6 = (bf16[8,112,256]{2,1,0:T(8,128)(2,1)S(1)}, bf16[8,112,256]{2,1,0:T(8,128)(2,1)S(1)}, u32[]{:S(2)}, u32[]{:S(2)}) collective-permute-start(bf16[8,112,256]{2,1,0:T(8,128)(2,1)S(1)} %all-to-all-done.own0), channel_id=1, source_target_pairs={{0,12},{4,0},{8,4},{12,8},{1,13},{5,1},{9,5},{13,9},{2,14},{6,2},{... | collective-permute-start | bytes 1376264 | tf_op jit(solution)/shard_map/ppermute | solution.py:29
  28.5 25.8 %collective-permute-start.2 = (bf16[8,112,256]{2,1,0:T(8,128)(2,1)S(1)}, bf16[8,112,256]{2,1,0:T(8,128)(2,1)S(1)}, u32[]{:S(2)}, u32[]{:S(2)}) collective-permute-start(bf16[8,112,256]{2,1,0:T(8,128)(2,1)S(1)} %all-to-all-done.own0), channel_id=1, source_target_pairs={{0,4},{4,8},{8,12},{12,0},{1,5},{5,9},{9,13},{13,1},{2,6},{6,10},{... | collective-permute-start | bytes 1376264 | tf_op jit(solution)/shard_map/ppermute | solution.py:29
  29.0 24.3 %collective-permute-start.5 = (bf16[96,2048]{1,0:T(8,128)(2,1)S(1)}, bf16[96,2048]{1,0:T(8,128)(2,1)}, u32[]{:S(2)}, u32[]{:S(2)}) collective-permute-start(bf16[96,2048]{1,0:T(8,128)(2,1)S(1)} %pad_maximum_fusion), channel_id=1, source_target_pairs={{0,128},{1,192},{2,0},{3,64},{64,129},{65,193},{66,1},{67,65},{128... | collective-permute-start | bytes 1179656 | tf_op jit(solution)/shard_map/ppermute | solution.py:29
  37.0 16.7 %collective-permute-start.4 = (bf16[96,2048]{1,0:T(8,128)(2,1)S(1)}, bf16[96,2048]{1,0:T(8,128)(2,1)}, u32[]{:S(2)}, u32[]{:S(2)}) collective-permute-start(bf16[96,2048]{1,0:T(8,128)(2,1)S(1)} %pad_maximum_fusion), channel_id=1, source_target_pairs={{0,0},{1,64},{2,128},{3,192},{64,1},{65,65},{66,129},{67,193},{128... | collective-permute-start | bytes 1179656 | tf_op jit(solution)/shard_map/ppermute | solution.py:29
  53.3 3.3 %collective-permute-start.7 = (bf16[8,112,256]{2,1,0:T(8,128)(2,1)S(1)}, bf16[8,112,256]{2,1,0:T(8,128)(2,1)S(1)}, u32[]{:S(2)}, u32[]{:S(2)}) collective-permute-start(bf16[8,112,256]{2,1,0:T(8,128)(2,1)S(1)} %all-to-all-done.own0), channel_id=1, source_target_pairs={{0,64},{64,0},{1,65},{65,1},{2,66},{66,2},{3,67},{67,3},{4,68},{68... | collective-permute-start | bytes 1376264 | tf_op jit(solution)/shard_map/ppermute | solution.py:29
  53.7 3.6 %copy-start.18 = (bf16[8,112,256]{2,1,0:T(8,128)(2,1)}, bf16[8,112,256]{2,1,0:T(8,128)(2,1)S(1)}, u32[]{:S(2)}) copy-start(bf16[8,112,256]{2,1,0:T(8,128)(2,1)S(1)} %collective-permute-done.3.own2) | copy-start | bytes 1376260
  53.7 3.5 %collective-permute-start.9 = (bf16[8,112,256]{2,1,0:T(8,128)(2,1)S(1)}, bf16[8,112,256]{2,1,0:T(8,128)(2,1)S(1)}, u32[]{:S(2)}, u32[]{:S(2)}) collective-permute-start(bf16[8,112,256]{2,1,0:T(8,128)(2,1)S(1)} %collective-permute-done.3.own2), channel_id=1, source_target_pairs={{0,64},{64,0},{1,65},{65,1},{2,66},{66,2},{3,67},{67,3},{4,68},{68... | collective-permute-start | bytes 1376264 | tf_op jit(solution)/shard_map/ppermute | solution.py:29
  54.0 3.3 %copy-start.19 = (bf16[8,112,256]{2,1,0:T(8,128)(2,1)}, bf16[8,112,256]{2,1,0:T(8,128)(2,1)S(1)}, u32[]{:S(2)}) copy-start(bf16[8,112,256]{2,1,0:T(8,128)(2,1)S(1)} %collective-permute-done.6.own3) | copy-start | bytes 1376260
  54.0 3.2 %collective-permute-start.10 = (bf16[8,112,256]{2,1,0:T(8,128)(2,1)S(1)}, bf16[8,112,256]{2,1,0:T(8,128)(2,1)S(1)}, u32[]{:S(2)}, u32[]{:S(2)}) collective-permute-start(bf16[8,112,256]{2,1,0:T(8,128)(2,1)S(1)} %collective-permute-done.6.own3), channel_id=1, source_target_pairs={{0,64},{64,0},{1,65},{65,1},{2,66},{66,2},{3,67},{67,3},{4,68},{68... | collective-permute-start | bytes 1376264 | tf_op jit(solution)/shard_map/ppermute | solution.py:29
  54.3 3.0 %copy-start.20 = (bf16[8,112,256]{2,1,0:T(8,128)(2,1)}, bf16[8,112,256]{2,1,0:T(8,128)(2,1)S(1)}, u32[]{:S(2)}) copy-start(bf16[8,112,256]{2,1,0:T(8,128)(2,1)S(1)} %collective-permute-done.2.own1) | copy-start | bytes 1376260
  54.3 3.0 %collective-permute-start.8 = (bf16[8,112,256]{2,1,0:T(8,128)(2,1)S(1)}, bf16[8,112,256]{2,1,0:T(8,128)(2,1)}, u32[]{:S(2)}, u32[]{:S(2)}) collective-permute-start(bf16[8,112,256]{2,1,0:T(8,128)(2,1)S(1)} %collective-permute-done.2.own1), channel_id=1, source_target_pairs={{0,64},{64,0},{1,65},{65,1},{2,66},{66,2},{3,67},{67,3},{4,68},{68... | collective-permute-start | bytes 1376264 | tf_op jit(solution)/shard_map/ppermute | solution.py:29
  56.6 36.7 %copy-start.15 = (f32[96]{0:T(128)S(1)}, f32[96]{0:T(128)}, u32[]{:S(2)}) copy-start(f32[96]{0:T(128)} %param.21) | copy-start | bytes 1156
  56.6 37.4 %copy-start.16 = (f32[96]{0:T(128)S(1)}, f32[96]{0:T(128)}, u32[]{:S(2)}) copy-start(f32[96]{0:T(128)} %param.22) | copy-start | bytes 1156
  56.6 0.8 copy-start.21
  57.1 0.8 copy-start.23
  57.1 0.9 copy-start.22
  67.1 14.9 %collective-permute-start.11 = (bf16[96,256]{1,0:T(8,128)(2,1)}, bf16[96,256]{1,0:T(8,128)(2,1)S(1)}, u32[]{:S(2)}, u32[]{:S(2)}) collective-permute-start(bf16[96,256]{1,0:T(8,128)(2,1)} %get-tuple-element.32), channel_id=1, source_target_pairs={{0,0},{16,32},{32,64},{48,96},{64,16},{80,48},{96,80},{112,112},{1... | collective-permute-start | bytes 147464 | tf_op jit(solution)/shard_map/ppermute | solution.py:29
  69.9 12.0 %collective-permute-start.12 = (bf16[96,256]{1,0:T(8,128)(2,1)}, bf16[96,256]{1,0:T(8,128)(2,1)S(1)}, u32[]{:S(2)}, u32[]{:S(2)}) collective-permute-start(bf16[96,256]{1,0:T(8,128)(2,1)} %get-tuple-element.33), channel_id=1, source_target_pairs={{0,64},{16,96},{32,0},{48,32},{64,80},{80,112},{96,16},{112,48},{1... | collective-permute-start | bytes 147464 | tf_op jit(solution)/shard_map/ppermute | solution.py:29
  71.0 12.6 %collective-permute-start.13 = (bf16[96,256]{1,0:T(8,128)(2,1)}, bf16[96,256]{1,0:T(8,128)(2,1)S(1)}, u32[]{:S(2)}, u32[]{:S(2)}) collective-permute-start(bf16[96,256]{1,0:T(8,128)(2,1)} %get-tuple-element.34), channel_id=1, source_target_pairs={{0,128},{16,160},{32,192},{48,224},{64,144},{80,176},{96,208},{112... | collective-permute-start | bytes 147464 | tf_op jit(solution)/shard_map/ppermute | solution.py:29
  79.1 6.7 %collective-permute-start.14 = (bf16[96,256]{1,0:T(8,128)(2,1)}, bf16[96,256]{1,0:T(8,128)(2,1)S(1)}, u32[]{:S(2)}, u32[]{:S(2)}) collective-permute-start(bf16[96,256]{1,0:T(8,128)(2,1)} %get-tuple-element.35), channel_id=1, source_target_pairs={{0,192},{16,224},{32,128},{48,160},{64,208},{80,240},{96,144},{112... | collective-permute-start | bytes 147464 | tf_op jit(solution)/shard_map/ppermute | solution.py:29
  82.0 3.8 %copy-start.8 = (bf16[96,256]{1,0:T(8,128)(2,1)}, bf16[96,256]{1,0:T(8,128)(2,1)S(1)}, u32[]{:S(2)}) copy-start(bf16[96,256]{1,0:T(8,128)(2,1)S(1)} %collective-permute-done.11.piece0) | copy-start | bytes 147460
  82.0 3.8 %copy-start.9 = (bf16[96,256]{1,0:T(8,128)(2,1)}, bf16[96,256]{1,0:T(8,128)(2,1)S(1)}, u32[]{:S(2)}) copy-start(bf16[96,256]{1,0:T(8,128)(2,1)S(1)} %collective-permute-done.12.piece1) | copy-start | bytes 147460
  83.6 2.2 %copy-start.10 = (bf16[96,256]{1,0:T(8,128)(2,1)}, bf16[96,256]{1,0:T(8,128)(2,1)S(1)}, u32[]{:S(2)}) copy-start(bf16[96,256]{1,0:T(8,128)(2,1)S(1)} %collective-permute-done.13.piece2) | copy-start | bytes 147460
  85.8 0.6 copy-start.11
  88.1 24.1 %collective-permute-start.18 = (bf16[96,2048]{1,0:T(8,128)(2,1)}, bf16[96,2048]{1,0:T(8,128)(2,1)S(1)}, u32[]{:S(2)}, u32[]{:S(2)}) collective-permute-start(bf16[96,2048]{1,0:T(8,128)(2,1)} %collective-permute-done.4.near0), channel_id=1, source_target_pairs={{0,64},{64,0},{1,65},{65,1},{2,66},{66,2},{3,67},{67,3},{4,68},{68... | collective-permute-start | bytes 1179656 | tf_op jit(solution)/shard_map/ppermute | solution.py:29
  89.7 22.6 %collective-permute-start.19 = (bf16[96,2048]{1,0:T(8,128)(2,1)}, bf16[96,2048]{1,0:T(8,128)(2,1)S(1)}, u32[]{:S(2)}, u32[]{:S(2)}) collective-permute-start(bf16[96,2048]{1,0:T(8,128)(2,1)} %collective-permute-done.5.near1), channel_id=1, source_target_pairs={{0,64},{64,0},{1,65},{65,1},{2,66},{66,2},{3,67},{67,3},{4,68},{68... | collective-permute-start | bytes 1179656 | tf_op jit(solution)/shard_map/ppermute | solution.py:29
  89.7 22.5 %collective-permute-start.17 = (bf16[96,1024]{1,0:T(8,128)(2,1)}, bf16[96,1024]{1,0:T(8,128)(2,1)S(1)}, u32[]{:S(2)}, u32[]{:S(2)}) collective-permute-start(bf16[96,1024]{1,0:T(8,128)(2,1)} %get-tuple-element.36.clip0.clip), channel_id=1, source_target_pairs={{0,3},{1,0},{2,1},{3,2},{4,7},{5,4},{6,5},{7,6},{8,11},{9,8},{10,9... | collective-permute-start | bytes 589832 | tf_op jit(solution)/shard_map/ppermute | solution.py:29
  91.2 20.9 %collective-permute-start.16 = (bf16[96,1024]{1,0:T(8,128)(2,1)}, bf16[96,1024]{1,0:T(8,128)(2,1)S(1)}, u32[]{:S(2)}, u32[]{:S(2)}) collective-permute-start(bf16[96,1024]{1,0:T(8,128)(2,1)} %get-tuple-element.36.clip0.clip), channel_id=1, source_target_pairs={{0,2},{1,3},{2,0},{3,1},{4,6},{5,7},{6,4},{7,5},{8,10},{9,11},{10,... | collective-permute-start | bytes 589832 | tf_op jit(solution)/shard_map/ppermute | solution.py:29
  92.4 19.8 %collective-permute-start.15 = (bf16[96,1024]{1,0:T(8,128)(2,1)}, bf16[96,1024]{1,0:T(8,128)(2,1)S(1)}, u32[]{:S(2)}, u32[]{:S(2)}) collective-permute-start(bf16[96,1024]{1,0:T(8,128)(2,1)} %get-tuple-element.36.clip0.clip), channel_id=1, source_target_pairs={{0,1},{1,2},{2,3},{3,0},{4,5},{5,6},{6,7},{7,4},{8,9},{9,10},{10,1... | collective-permute-start | bytes 589832 | tf_op jit(solution)/shard_map/ppermute | solution.py:29
  94.7 17.4 %all-to-all-start.1 = ((f32[64,1,128]{2,1,0:T(1,128)}), f32[64,1,128]{2,1,0:T(1,128)S(1)}, u32[]{:S(2)}, u32[]{:S(2)}) async-start(f32[64,1,128]{2,1,0:T(1,128)} %get-tuple-element.37), calls=%async_computation.1 | async-start | bytes 65536 | tf_op jit(solution)/shard_map/all_to_all | solution.py:450
  112.2 0.6 copy-start.12
  112.2 0.7 copy-start.26
  112.2 0.7 copy-start.27
  112.2 0.8 copy-start.28
  112.2 0.9 copy-start.24
  112.2 1.0 copy-start.25
  113.2 18.3 %copy-start.1 = (bf16[3,3,3,96,384]{4,3,2,1,0:T(8,128)(2,1)S(1)}, bf16[3,3,3,96,384]{4,3,2,1,0:T(8,128)(2,1)}, u32[]{:S(2)}) copy-start(bf16[3,3,3,96,384]{4,3,2,1,0:T(8,128)(2,1)} %param.23) | copy-start | bytes 5971972
  119.8 14.1 %collective-permute-start.20 = (bf16[96,512]{1,0:T(8,128)(2,1)}, bf16[96,512]{1,0:T(8,128)(2,1)S(1)}, u32[]{:S(2)}, u32[]{:S(2)}) collective-permute-start(bf16[96,512]{1,0:T(8,128)(2,1)} %get-tuple-element.45), channel_id=1, source_target_pairs={{0,4},{4,8},{8,12},{12,16},{16,20},{20,24},{24,28},{28,32},{32,36}... | collective-permute-start | bytes 294920 | tf_op jit(solution)/shard_map/ppermute | solution.py:29
  122.0 11.9 %collective-permute-start.21 = (bf16[96,512]{1,0:T(8,128)(2,1)}, bf16[96,512]{1,0:T(8,128)(2,1)S(1)}, u32[]{:S(2)}, u32[]{:S(2)}) collective-permute-start(bf16[96,512]{1,0:T(8,128)(2,1)} %get-tuple-element.46), channel_id=1, source_target_pairs={{4,0},{8,4},{12,8},{16,12},{20,16},{24,20},{28,24},{32,28},{36,32}... | collective-permute-start | bytes 294920 | tf_op jit(solution)/shard_map/ppermute | solution.py:29
  127.7 19.9 %all-to-all-start.2 = ((bf16[16,8,16,128]{3,2,1,0:T(8,128)(2,1)}), bf16[16,8,16,128]{3,2,1,0:T(8,128)(2,1)S(1)}, u32[]{:S(2)}, u32[]{:S(2)}) async-start(bf16[16,8,16,128]{3,2,1,0:T(8,128)(2,1)} %bitcast.48), calls=%async_computation.2 | async-start | bytes 1048576 | tf_op jit(solution)/shard_map/all_to_all | solution.py:473
  133.9 0.6 copy-start.29
  134.5 0.6 copy-start.30
  141.0 5.4 %collective-permute-start.22 = (bf16[2,96,1024]{2,1,0:T(8,128)(2,1)}, bf16[2,96,1024]{2,1,0:T(8,128)(2,1)S(1)}, u32[]{:S(2)}, u32[]{:S(2)}) collective-permute-start(bf16[2,96,1024]{2,1,0:T(8,128)(2,1)} %get-tuple-element.49), channel_id=1, source_target_pairs={{0,64},{64,0},{1,65},{65,1},{2,66},{66,2},{3,67},{67,3},{4,68},{68... | collective-permute-start | bytes 1179656 | tf_op jit(solution)/shard_map/ppermute | solution.py:29
  147.5 35.9 %copy-start.7 = (bf16[96,1024]{1,0:T(8,128)(2,1)S(1)}, bf16[96,1024]{1,0:T(8,128)(2,1)}, u32[]{:S(2)}) copy-start(bf16[96,1024]{1,0:T(8,128)(2,1)} %get-tuple-element.36.clip0.clip) | copy-start | bytes 589828
  147.6 35.8 %copy-start.17 = (f32[96]{0:T(128)S(1)}, f32[96]{0:T(128)}, u32[]{:S(2)}) copy-start(f32[96]{0:T(128)} %param.24) | copy-start | bytes 1156
  169.2 29.3 %copy-start = (bf16[16,8,16,128]{3,2,1,0:T(8,128)(2,1)}, bf16[16,8,16,128]{3,2,1,0:T(8,128)(2,1)S(1)}, u32[]{:S(2)}) copy-start(bf16[16,8,16,128]{3,2,1,0:T(8,128)(2,1)S(1)} %all_to_all.20) | copy-start | bytes 1572868
  169.2 14.2 %collective-permute-start.23 = (bf16[96,1024]{1,0:T(8,128)(2,1)S(1)}, bf16[96,1024]{1,0:T(8,128)(2,1)S(1)}, u32[]{:S(2)}, u32[]{:S(2)}) collective-permute-start(bf16[96,1024]{1,0:T(8,128)(2,1)S(1)} %fusion.1), channel_id=1, source_target_pairs={{0,128},{128,0},{1,129},{129,1},{2,130},{130,2},{3,131},{131,3},{4... | collective-permute-start | bytes 589832 | tf_op jit(solution)/shard_map/ppermute | solution.py:29
  171.1 13.7 %collective-permute-start.26 = (bf16[128,16,128]{2,1,0:T(8,128)(2,1)S(1)}, bf16[128,16,128]{2,1,0:T(8,128)(2,1)S(1)}, u32[]{:S(2)}, u32[]{:S(2)}) collective-permute-start(bf16[128,16,128]{2,1,0:T(8,128)(2,1)S(1)} %bitcast.43), channel_id=1, source_target_pairs={{0,3},{1,0},{2,1},{3,2},{4,7},{5,4},{6,5},{7,6},{8,11},{9,8},{10,9... | collective-permute-start | bytes 1572872 | tf_op jit(solution)/shard_map/ppermute | solution.py:29
  172.0 13.3 %collective-permute-start.25 = (bf16[128,16,128]{2,1,0:T(8,128)(2,1)S(1)}, bf16[128,16,128]{2,1,0:T(8,128)(2,1)S(1)}, u32[]{:S(2)}, u32[]{:S(2)}) collective-permute-start(bf16[128,16,128]{2,1,0:T(8,128)(2,1)S(1)} %bitcast.44), channel_id=1, source_target_pairs={{0,2},{1,3},{2,0},{3,1},{4,6},{5,7},{6,4},{7,5},{8,10},{9,11},{10,... | collective-permute-start | bytes 1572872 | tf_op jit(solution)/shard_map/ppermute | solution.py:29
  173.1 25.4 %collective-permute-start.24 = (bf16[128,16,128]{2,1,0:T(8,128)(2,1)S(1)}, bf16[128,16,128]{2,1,0:T(8,128)(2,1)S(1)}, u32[]{:S(2)}, u32[]{:S(2)}) collective-permute-start(bf16[128,16,128]{2,1,0:T(8,128)(2,1)S(1)} %bitcast.45), channel_id=1, source_target_pairs={{0,1},{1,2},{2,3},{3,0},{4,5},{5,6},{6,7},{7,4},{8,9},{9,10},{10,1... | collective-permute-start | bytes 1572872 | tf_op jit(solution)/shard_map/ppermute | solution.py:29
  184.7 13.8 %copy-start.3 = (bf16[128,16,128]{2,1,0:T(8,128)(2,1)}, bf16[128,16,128]{2,1,0:T(8,128)(2,1)S(1)}, u32[]{:S(2)}) copy-start(bf16[128,16,128]{2,1,0:T(8,128)(2,1)S(1)} %collective-permute-done.26.table3) | copy-start | bytes 1572868
  185.2 13.3 %copy-start.4 = (bf16[128,16,128]{2,1,0:T(8,128)(2,1)}, bf16[128,16,128]{2,1,0:T(8,128)(2,1)S(1)}, u32[]{:S(2)}) copy-start(bf16[128,16,128]{2,1,0:T(8,128)(2,1)S(1)} %collective-permute-done.25.table2) | copy-start | bytes 1572868
  198.6 0.8 copy-start.5
where the time goes:
time: 206 us; the launch traced here: 204 us
  starting transfers between devices  76.4 us (37%)
  waiting for transfers between devices  56.9 us (28%)
  Pallas kernels  29.3 us (14%)
  blocking collectives  21.4 us (10%)
  local copies, waits for them, and re-layouts  13.3 us (6%)
  other arithmetic  4.88 us (2%)
    ppermute x27, starting transfers between devices, permute(): return lax.ppermute(value, axes, pairs)  54.6 us
    ppermute x27, waiting for transfers between devices, permute(): return lax.ppermute(value, axes, pairs)  50.4 us
    all_to_all x1, blocking collectives, spread(): return lax.all_to_all(copies, axes, 0, 0, tiled=True)  21.4 us
    all_to_all x1, starting transfers between devices, body(): packed = lax.all_to_all(packed, ('zl', 'x', 'y'), 0, 0, tiled=True)  10.4 us
    pallas_call x1, Pallas kernels, body(): pl.pallas_call(attend_kernel, out_shape=[jax.ShapeDtypeStruct((96, 256),...  9 us
    all_to_all x1, starting transfers between devices, body(): mine = lax.all_to_all(by_frame, ('zh', 'zl'), 0, 0, tiled=True)  7.69 us
    pallas_call x1, Pallas kernels, body(): pl.pallas_call(grad_kernel, out_shape=jax.ShapeDtypeStruct((128, 16, 128)...  6.52 us
    all_to_all x1, waiting for transfers between devices, body(): packed = lax.all_to_all(packed, ('zl', 'x', 'y'), 0, 0, tiled=True)  6.47 us
  transfers between devices with their start and end apart: 30, of which 12 were waited for; matrix products, arithmetic and copies ran while one was open for 6% of the time, Pallas kernels for 3%

commit v1 on v0

--- a/solution.py
+++ b/solution.py
@@ -290,14 +290,11 @@
     out[126:] = jnp.zeros((2, 16, 128), BF)
 
 
-def join_kernel(at, table0, table1, table2, table3, out, held):
-    for s, table in enumerate((table0, table1, table2, table3)):
-        held[lax.rem(at[0] - s + 4, 4)] = table[...]
+def join_kernel(tables, out):
     for ky in range(3):
         for l in range(7):
-            blocks = [
-                held[j, (ky * 6 + t) * 7 + l] for j in range(4) for t in range(6)
-            ]
+            tiles = [(ky * 6 + t) * 7 + l for t in range(6)]
+            blocks = [tables[j, t] for j in range(4) for t in tiles]
             flipped = jnp.concatenate(blocks, axis=0).astype(F32).T
             lane = l * 128
             while lane < min(l * 128 + 128, 864):
@@ -501,13 +498,10 @@
     weight_grad = pl.pallas_call(
         join_kernel,
         out_shape=jax.ShapeDtypeStruct((2592, 384), F32),
-        in_specs=[scalars] + [whole] * 4,
-        out_specs=whole,
-        scratch_shapes=[pltpu.VMEM((4, 128, 16, 128), BF)],
         compiler_params=params,
         cost_estimate=cost(10**6, 6 * 10**6),
         name="join",
-    )(y.astype(jnp.int32)[None], *ring(table, "y"))
+    )(spread(table, ("y",), 4).reshape(4, 128, 16, 128))
     weight_grad = weight_grad.reshape(3, 3, 3, 96, 384)
 
     conv = near + permute(far, ("zh",), lambda i: (1 - i,)).astype(F32)

time: 206 us -> 207 us (level)
  waiting for transfers between devices: 56.9 us -> 54.7 us
    ppermute x27 -> x24, waiting for transfers between devices: 50.4 us -> 38.7 us  [permute(): return lax.ppermute(value, axes, pairs)]
    all_to_all x0 -> x1, waiting for transfers between devices: none -> 9.59 us  [spread(): return lax.all_to_all(copies, axes, 0, 0, tiled=True)]
    all_to_all x0 -> x1, starting transfers between devices: none -> 3.74 us  [spread(): return lax.all_to_all(copies, axes, 0, 0, tiled=True)]
    ppermute x27 -> x24, starting transfers between devices: 54.6 us -> 52.7 us  [permute(): return lax.ppermute(value, axes, pairs)]
    unnamed x66 -> x60, local copies, waits for them, and re-layouts: 4.65 us -> 4.68 us
  transfers between devices with their start and end apart: 30 -> 28, of which waited for: 12 -> 10; matrix products, arithmetic and copies ran while one was open for 6% -> 6% of each run, Pallas kernels for 3% -> 3%
where the time goes in v1:
time: 207 us; the launch traced here: 205 us
  starting transfers between devices  78.2 us (38%)
  waiting for transfers between devices  54.7 us (26%)
  Pallas kernels  29.1 us (14%)
  blocking collectives  21.4 us (10%)
  local copies, waits for them, and re-layouts  14.9 us (7%)
  other arithmetic  4.94 us (2%)
    ppermute x24, starting transfers between devices, permute(): return lax.ppermute(value, axes, pairs)  52.7 us
    ppermute x24, waiting for transfers between devices, permute(): return lax.ppermute(value, axes, pairs)  38.7 us
    all_to_all x1, blocking collectives, spread(): return lax.all_to_all(copies, axes, 0, 0, tiled=True)  21.4 us
    all_to_all x1, starting transfers between devices, body(): packed = lax.all_to_all(packed, ('zl', 'x', 'y'), 0, 0, tiled=True)  10.3 us
    all_to_all x1, waiting for transfers between devices, spread(): return lax.all_to_all(copies, axes, 0, 0, tiled=True)  9.59 us
    pallas_call x1, Pallas kernels, body(): pl.pallas_call(attend_kernel, out_shape=[jax.ShapeDtypeStruct((96, 256),...  9.01 us
    all_to_all x1, starting transfers between devices, body(): mine = lax.all_to_all(by_frame, ('zh', 'zl'), 0, 0, tiled=True)  7.69 us
    pallas_call x1, Pallas kernels, body(): pl.pallas_call(grad_kernel, out_shape=jax.ShapeDtypeStruct((128, 16, 128)...  6.5 us
  transfers between devices with their start and end apart: 28, of which 10 were waited for; matrix products, arithmetic and copies ran while one was open for 6% of the time, Pallas kernels for 3%

profile of v1, /device:TPU:65, one launch (start us, length us, event | category | flops | bytes accessed | tf_op | source)
XLA Modules:
  0.0 205.0 jit_solution(2102586470689812861)
XLA Ops:
  1.3 1.7 reshape.60.frames
  3.0 1.9 pack.1
  4.9 7.7 %all-to-all-start = ((bf16[8,112,256]{2,1,0:T(8,128)(2,1)}), bf16[8,112,256]{2,1,0:T(8,128)(2,1)S(1)}, u32[]{:S(2)}, u32[]{:S(2)}) async-start(bf16[8,112,256]{2,1,0:T(8,128)(2,1)} %pack.1), calls=%async_computation | async-start | bytes 917504 | tf_op jit(solution)/shard_map/all_to_all | solution.py:376
  12.9 1.1 slice_reduce_fusion.1
  14.0 4.4 %collective-permute-start.1 = (bf16[96,512]{1,0:T(8,128)(2,1)S(1)}, bf16[96,512]{1,0:T(8,128)(2,1)S(1)}, u32[]{:S(2)}, u32[]{:S(2)}) collective-permute-start(bf16[96,512]{1,0:T(8,128)(2,1)S(1)} %bitcast.48), channel_id=1, source_target_pairs={{4,0},{8,4},{12,8},{16,12},{20,16},{24,20},{28,24},{32,28},{36,32}... | collective-permute-start | bytes 294920 | tf_op jit(solution)/shard_map/ppermute | solution.py:29
  18.4 1.9 collective-permute-start
  20.6 2.2 %collective-permute-done.1 = bf16[96,512]{1,0:T(8,128)(2,1)S(1)} collective-permute-done((bf16[96,512]{1,0:T(8,128)(2,1)S(1)}, bf16[96,512]{1,0:T(8,128)(2,1)S(1)}, u32[]{:S(2)}, u32[]{:S(2)}) %collective-permute-start.1) | collective-permute-done | bytes 98336 | tf_op jit(solution)/shard_map/ppermute | solution.py:29
  22.8 3.6 %collective-permute-done = bf16[96,512]{1,0:T(8,128)(2,1)S(1)} collective-permute-done((bf16[96,512]{1,0:T(8,128)(2,1)S(1)}, bf16[96,512]{1,0:T(8,128)(2,1)S(1)}, u32[]{:S(2)}, u32[]{:S(2)}) %collective-permute-start) | collective-permute-done | bytes 98336 | tf_op jit(solution)/shard_map/ppermute | solution.py:29
  26.5 0.7 collective-permute-start.3
  27.2 1.3 collective-permute-start.6
  28.5 0.5 collective-permute-start.2
  29.0 8.0 %collective-permute-start.5 = (bf16[96,2048]{1,0:T(8,128)(2,1)S(1)}, bf16[96,2048]{1,0:T(8,128)(2,1)S(1)}, u32[]{:S(2)}, u32[]{:S(2)}) collective-permute-start(bf16[96,2048]{1,0:T(8,128)(2,1)S(1)} %pad_maximum_fusion), channel_id=1, source_target_pairs={{0,128},{1,192},{2,0},{3,64},{64,129},{65,193},{66,1},{67,65},{128... | collective-permute-start | bytes 1179656 | tf_op jit(solution)/shard_map/ppermute | solution.py:29
  37.0 1.9 collective-permute-start.4
  38.9 14.4 %collective-permute-done.5.near1 = bf16[96,2048]{1,0:T(8,128)(2,1)S(1)} collective-permute-done((bf16[96,2048]{1,0:T(8,128)(2,1)S(1)}, bf16[96,2048]{1,0:T(8,128)(2,1)S(1)}, u32[]{:S(2)}, u32[]{:S(2)}) %collective-permute-start.5) | collective-permute-done | bytes 393248 | tf_op jit(solution)/shard_map/ppermute | solution.py:29
  53.3 0.3 collective-permute-start.7
  53.7 0.3 collective-permute-start.9
  54.0 0.3 collective-permute-start.10
  54.3 0.3 collective-permute-start.8
  54.6 0.6 broadcast_in_dim.35.qkv_bias
  55.2 0.8 broadcast_in_dim.41.out_bias
  56.0 0.7 pad_add_fusion.1.at
  56.7 0.6 collective-permute-done.8.other1
  57.6 9.0 %attention.1 = (bf16[96,256]{1,0:T(8,128)(2,1)}, bf16[96,256]{1,0:T(8,128)(2,1)}, bf16[96,256]{1,0:T(8,128)(2,1)}, bf16[96,256]{1,0:T(8,128)(2,1)}) custom-call(s32[4]{0:T(128)} %pad_add_fusion.1.at, bf16[8,112,256]{2,1,0:T(8,128)(2,1)} %copy-done.3, bf16[8,112,256]{2,1,0:T(8,128)(2,1)} %copy-done.17, bf16[8,112,256]{2,1,0:T(8,128)(2,1)} %copy-done.15, ...), custom_call_target="tpu_custom_call" | custom-call | flops 4000000000 | bytes 20000000 | tf_op jit(solution)/shard_map/attention/pallas_call | solution.py:396
  66.6 2.8 %collective-permute-start.11 = (bf16[96,256]{1,0:T(8,128)(2,1)}, bf16[96,256]{1,0:T(8,128)(2,1)S(1)}, u32[]{:S(2)}, u32[]{:S(2)}) collective-permute-start(bf16[96,256]{1,0:T(8,128)(2,1)} %get-tuple-element.32), channel_id=1, source_target_pairs={{0,0},{16,32},{32,64},{48,96},{64,16},{80,48},{96,80},{112,112},{1... | collective-permute-start | bytes 147464 | tf_op jit(solution)/shard_map/ppermute | solution.py:29
  69.4 1.1 collective-permute-start.12
  70.4 8.5 %collective-permute-start.13 = (bf16[96,256]{1,0:T(8,128)(2,1)}, bf16[96,256]{1,0:T(8,128)(2,1)S(1)}, u32[]{:S(2)}, u32[]{:S(2)}) collective-permute-start(bf16[96,256]{1,0:T(8,128)(2,1)} %get-tuple-element.34), channel_id=1, source_target_pairs={{0,128},{16,160},{32,192},{48,224},{64,144},{80,176},{96,208},{112... | collective-permute-start | bytes 147464 | tf_op jit(solution)/shard_map/ppermute | solution.py:29
  78.9 2.2 %collective-permute-start.14 = (bf16[96,256]{1,0:T(8,128)(2,1)}, bf16[96,256]{1,0:T(8,128)(2,1)S(1)}, u32[]{:S(2)}, u32[]{:S(2)}) collective-permute-start(bf16[96,256]{1,0:T(8,128)(2,1)} %get-tuple-element.35), channel_id=1, source_target_pairs={{0,192},{16,224},{32,128},{48,160},{64,208},{80,240},{96,144},{112... | collective-permute-start | bytes 147464 | tf_op jit(solution)/shard_map/ppermute | solution.py:29
  81.1 0.6 pad_add_fusion.at
  81.7 1.6 collective-permute-done.13.piece2
  83.4 2.3 %collective-permute-done.14.piece3 = bf16[96,256]{1,0:T(8,128)(2,1)S(1)} collective-permute-done((bf16[96,256]{1,0:T(8,128)(2,1)}, bf16[96,256]{1,0:T(8,128)(2,1)S(1)}, u32[]{:S(2)}, u32[]{:S(2)}) %collective-permute-start.14) | collective-permute-done | bytes 49184 | tf_op jit(solution)/shard_map/ppermute | solution.py:29
  85.7 0.6 copy-done.8
  86.3 1.7 arrange.1
  88.0 1.4 collective-permute-start.18
  89.5 1.5 collective-permute-start.17
  91.0 1.3 collective-permute-start.16
  92.3 0.9 collective-permute-start.15
  93.1 0.7 copy.22.gain
  93.9 0.7 copy.23.shift
  94.6 10.3 %all-to-all-start.1 = ((f32[64,1,128]{2,1,0:T(1,128)}), f32[64,1,128]{2,1,0:T(1,128)S(1)}, u32[]{:S(2)}, u32[]{:S(2)}) async-start(f32[64,1,128]{2,1,0:T(1,128)} %get-tuple-element.37), calls=%async_computation.1 | async-start | bytes 65536 | tf_op jit(solution)/shard_map/all_to_all | solution.py:447
  104.9 0.6 pad_add_fusion.2.at
  105.5 6.4 %all-to-all-done.1 = f32[64,1,128]{2,1,0:T(1,128)S(1)} async-done(((f32[64,1,128]{2,1,0:T(1,128)}), f32[64,1,128]{2,1,0:T(1,128)S(1)}, u32[]{:S(2)}, u32[]{:S(2)}) %all-to-all-start.1) | async-done | bytes 32800 | tf_op jit(solution)/shard_map/all_to_all | solution.py:447
  112.0 0.5 copy-done.9
  113.1 6.5 %weight_grad.1 = bf16[128,16,128]{2,1,0:T(8,128)(2,1)} custom-call(s32[3]{0:T(128)} %pad_add_fusion.2.at, f32[16,4,1,128]{3,2,1,0:T(1,128)} %bitcast.50, bf16[96,1024]{1,0:T(8,128)(2,1)} %get-tuple-element.36.clip0.clip, bf16[96,1024]{1,0:T(8,128)(2,1)} %copy-done.25, bf16[96,1024]{1,0:T(8,128)(2,1)} %copy-done.24, bf16[96,1024]{1,0:T(8,128)(2,1)} %copy-done.23, ...), custom_call_target="tpu_custom_call" | custom-call | flops 4000000000 | bytes 20000000 | tf_op jit(solution)/shard_map/weight_grad/pallas_call | solution.py:451
  119.6 2.2 %collective-permute-start.20 = (bf16[96,512]{1,0:T(8,128)(2,1)}, bf16[96,512]{1,0:T(8,128)(2,1)S(1)}, u32[]{:S(2)}, u32[]{:S(2)}) collective-permute-start(bf16[96,512]{1,0:T(8,128)(2,1)} %get-tuple-element.45), channel_id=1, source_target_pairs={{0,4},{4,8},{8,12},{12,16},{16,20},{20,24},{24,28},{28,32},{32,36}... | collective-permute-start | bytes 294920 | tf_op jit(solution)/shard_map/ppermute | solution.py:29
  121.8 5.2 %collective-permute-start.21 = (bf16[96,512]{1,0:T(8,128)(2,1)}, bf16[96,512]{1,0:T(8,128)(2,1)S(1)}, u32[]{:S(2)}, u32[]{:S(2)}) collective-permute-start(bf16[96,512]{1,0:T(8,128)(2,1)} %get-tuple-element.46), channel_id=1, source_target_pairs={{4,0},{8,4},{12,8},{16,12},{20,16},{24,20},{28,24},{32,28},{36,32}... | collective-permute-start | bytes 294920 | tf_op jit(solution)/shard_map/ppermute | solution.py:29
  127.0 0.6 pad_add_fusion.3.at
  127.6 3.8 %all-to-all-start.2 = ((bf16[16,8,16,128]{3,2,1,0:T(8,128)(2,1)}), bf16[16,8,16,128]{3,2,1,0:T(8,128)(2,1)S(1)}, u32[]{:S(2)}, u32[]{:S(2)}) async-start(bf16[16,8,16,128]{3,2,1,0:T(8,128)(2,1)} %bitcast.45), calls=%async_computation.2 | async-start | bytes 1048576 | tf_op jit(solution)/shard_map/all_to_all | solution.py:470
  131.3 2.4 %copy.24.weight = bf16[3,384,864]{2,1,0:T(8,128)(2,1)} copy(bf16[3,384,864]{1,2,0:T(8,128)(2,1)S(1)} %bitcast.44) | data formatting | bytes 3981312 | tf_op jit(solution)/shard_map/reshape | solution.py:469
  133.8 0.6 copy-done.26
  134.4 0.6 copy-done.27
  135.0 5.9 %convolution.1 = (bf16[2,96,1024]{2,1,0:T(8,128)(2,1)}, bf16[2,96,1024]{2,1,0:T(8,128)(2,1)}) custom-call(s32[3]{0:T(128)} %pad_add_fusion.3.at, f32[16,4,1,128]{3,2,1,0:T(1,128)} %bitcast.51, bf16[96,1024]{1,0:T(8,128)(2,1)} %get-tuple-element.36.clip0.clip, bf16[96,512]{1,0:T(8,128)(2,1)} %copy-done.26, bf16[96,512]{1,0:T(8,128)(2,1)} %copy-done.27, ...), custom_call_target="tpu_custom_call" | custom-call | flops 3000000000 | bytes 12000000 | tf_op jit(solution)/shard_map/convolution/pallas_call | solution.py:471
  140.9 3.8 %collective-permute-start.22 = (bf16[2,96,1024]{2,1,0:T(8,128)(2,1)}, bf16[2,96,1024]{2,1,0:T(8,128)(2,1)S(1)}, u32[]{:S(2)}, u32[]{:S(2)}) collective-permute-start(bf16[2,96,1024]{2,1,0:T(8,128)(2,1)} %get-tuple-element.49), channel_id=1, source_target_pairs={{0,64},{64,0},{1,65},{65,1},{2,66},{66,2},{3,67},{67,3},{4,68},{68... | collective-permute-start | bytes 1179656 | tf_op jit(solution)/shard_map/ppermute | solution.py:29
  144.7 1.6 collective-permute-done.22
  146.2 1.1 convert_add_fusion
  147.6 21.4 %all_to_all.25 = bf16[16,8,16,128]{3,2,1,0:T(8,128)(2,1)S(1)} all-to-all(bf16[16,8,16,128]{3,2,1,0:T(8,128)(2,1)S(1)} %broadcast_in_dim.39), channel_id=1, replica_groups=mesh['zh'=2,'co'=2,'zl'=4,'x'=4,'y'=4] {'zl','x'}, dimensions={0} | all-to-all | bytes 1048576 | tf_op jit(solution)/shard_map/all_to_all | solution.py:50
  169.0 1.6 broadcast_in_dim.40
  170.6 3.7 %all-to-all-start.4 = ((bf16[4,128,16,128]{3,2,1,0:T(8,128)(2,1)}), bf16[4,128,16,128]{3,2,1,0:T(8,128)(2,1)S(1)}, u32[]{:S(2)}, u32[]{:S(2)}) async-start(bf16[4,128,16,128]{3,2,1,0:T(8,128)(2,1)} %broadcast_in_dim.40), calls=%async_computation.4 | async-start | bytes 4194304 | tf_op jit(solution)/shard_map/all_to_all | solution.py:50
  174.3 1.9 collective-permute-start.23
  176.3 12.3 %collective-permute-done.23 = bf16[96,1024]{1,0:T(8,128)(2,1)S(1)} collective-permute-done((bf16[96,1024]{1,0:T(8,128)(2,1)S(1)}, bf16[96,1024]{1,0:T(8,128)(2,1)S(1)}, u32[]{:S(2)}, u32[]{:S(2)}) %collective-permute-start.23) | collective-permute-done | bytes 196640 | tf_op jit(solution)/shard_map/ppermute | solution.py:29
  188.7 0.3 reshape.67
  189.0 0.9 fusion
  189.9 9.6 %all-to-all-done.4.tables = bf16[4,128,16,128]{3,2,1,0:T(8,128)(2,1)S(1)} async-done(((bf16[4,128,16,128]{3,2,1,0:T(8,128)(2,1)}), bf16[4,128,16,128]{3,2,1,0:T(8,128)(2,1)S(1)}, u32[]{:S(2)}, u32[]{:S(2)}) %all-to-all-start.4) | async-done | bytes 2097184 | tf_op jit(solution)/shard_map/all_to_all | solution.py:50
  199.5 1.3 copy-done
  200.9 4.1 %join.1 = f32[2592,384]{1,0:T(8,128)} custom-call(bf16[4,128,16,128]{3,2,1,0:T(8,128)(2,1)} %copy-done), custom_call_target="tpu_custom_call" | custom-call | flops 1000000 | bytes 6000000 | tf_op jit(solution)/shard_map/join/pallas_call | solution.py:498
  (85 shorter events, 1.9 us)
Async XLA Ops:
  0.6 12.0 %copy-start.2 = (bf16[96,1,4,2,128]{4,3,2,1,0:T(2,128)(2,1)S(1)}, bf16[96,1,4,2,128]{4,3,2,1,0:T(2,128)(2,1)}, u32[]{:S(2)}) copy-start(bf16[96,1,4,2,128]{4,3,2,1,0:T(2,128)(2,1)} %param.25) | copy-start | bytes 589828
  4.9 49.7 %copy-start.10 = (f32[1152]{0:T(1024)S(1)}, f32[1152]{0:T(1024)}, u32[]{:S(2)}) copy-start(f32[1152]{0:T(1024)} %param.18) | copy-start | bytes 13828
  4.9 50.2 %copy-start.11 = (f32[384]{0:T(512)S(1)}, f32[384]{0:T(512)}, u32[]{:S(2)}) copy-start(f32[384]{0:T(512)} %param.20) | copy-start | bytes 4612
  4.9 21.5 %all-to-all-start = ((bf16[8,112,256]{2,1,0:T(8,128)(2,1)}), bf16[8,112,256]{2,1,0:T(8,128)(2,1)S(1)}, u32[]{:S(2)}, u32[]{:S(2)}) async-start(bf16[8,112,256]{2,1,0:T(8,128)(2,1)} %pack.1), calls=%async_computation | async-start | bytes 917504 | tf_op jit(solution)/shard_map/all_to_all | solution.py:376
  14.0 8.8 %collective-permute-start.1 = (bf16[96,512]{1,0:T(8,128)(2,1)S(1)}, bf16[96,512]{1,0:T(8,128)(2,1)S(1)}, u32[]{:S(2)}, u32[]{:S(2)}) collective-permute-start(bf16[96,512]{1,0:T(8,128)(2,1)S(1)} %bitcast.48), channel_id=1, source_target_pairs={{4,0},{8,4},{12,8},{16,12},{20,16},{24,20},{28,24},{32,28},{36,32}... | collective-permute-start | bytes 294920 | tf_op jit(solution)/shard_map/ppermute | solution.py:29
  18.4 8.0 %collective-permute-start = (bf16[96,512]{1,0:T(8,128)(2,1)S(1)}, bf16[96,512]{1,0:T(8,128)(2,1)S(1)}, u32[]{:S(2)}, u32[]{:S(2)}) collective-permute-start(bf16[96,512]{1,0:T(8,128)(2,1)S(1)} %bitcast.49), channel_id=1, source_target_pairs={{0,4},{4,8},{8,12},{12,16},{16,20},{20,24},{24,28},{28,32},{32,36}... | collective-permute-start | bytes 294920 | tf_op jit(solution)/shard_map/ppermute | solution.py:29
  26.5 30.8 %copy-start.3 = (bf16[8,112,256]{2,1,0:T(8,128)(2,1)}, bf16[8,112,256]{2,1,0:T(8,128)(2,1)S(1)}, u32[]{:S(2)}) copy-start(bf16[8,112,256]{2,1,0:T(8,128)(2,1)S(1)} %all-to-all-done.own0) | copy-start | bytes 1376260
  26.5 27.2 %collective-permute-start.3 = (bf16[8,112,256]{2,1,0:T(8,128)(2,1)S(1)}, bf16[8,112,256]{2,1,0:T(8,128)(2,1)S(1)}, u32[]{:S(2)}, u32[]{:S(2)}) collective-permute-start(bf16[8,112,256]{2,1,0:T(8,128)(2,1)S(1)} %all-to-all-done.own0), channel_id=1, source_target_pairs={{0,8},{4,12},{8,0},{12,4},{1,9},{5,13},{9,1},{13,5},{2,10},{6,14},... | collective-permute-start | bytes 1376264 | tf_op jit(solution)/shard_map/ppermute | solution.py:29
  27.2 26.7 %collective-permute-start.6 = (bf16[8,112,256]{2,1,0:T(8,128)(2,1)S(1)}, bf16[8,112,256]{2,1,0:T(8,128)(2,1)S(1)}, u32[]{:S(2)}, u32[]{:S(2)}) collective-permute-start(bf16[8,112,256]{2,1,0:T(8,128)(2,1)S(1)} %all-to-all-done.own0), channel_id=1, source_target_pairs={{0,12},{4,0},{8,4},{12,8},{1,13},{5,1},{9,5},{13,9},{2,14},{6,2},{... | collective-permute-start | bytes 1376264 | tf_op jit(solution)/shard_map/ppermute | solution.py:29
  28.5 25.8 %collective-permute-start.2 = (bf16[8,112,256]{2,1,0:T(8,128)(2,1)S(1)}, bf16[8,112,256]{2,1,0:T(8,128)(2,1)S(1)}, u32[]{:S(2)}, u32[]{:S(2)}) collective-permute-start(bf16[8,112,256]{2,1,0:T(8,128)(2,1)S(1)} %all-to-all-done.own0), channel_id=1, source_target_pairs={{0,4},{4,8},{8,12},{12,0},{1,5},{5,9},{9,13},{13,1},{2,6},{6,10},{... | collective-permute-start | bytes 1376264 | tf_op jit(solution)/shard_map/ppermute | solution.py:29
  29.0 24.3 %collective-permute-start.5 = (bf16[96,2048]{1,0:T(8,128)(2,1)S(1)}, bf16[96,2048]{1,0:T(8,128)(2,1)S(1)}, u32[]{:S(2)}, u32[]{:S(2)}) collective-permute-start(bf16[96,2048]{1,0:T(8,128)(2,1)S(1)} %pad_maximum_fusion), channel_id=1, source_target_pairs={{0,128},{1,192},{2,0},{3,64},{64,129},{65,193},{66,1},{67,65},{128... | collective-permute-start | bytes 1179656 | tf_op jit(solution)/shard_map/ppermute | solution.py:29
  37.0 16.7 %collective-permute-start.4 = (bf16[96,2048]{1,0:T(8,128)(2,1)S(1)}, bf16[96,2048]{1,0:T(8,128)(2,1)}, u32[]{:S(2)}, u32[]{:S(2)}) collective-permute-start(bf16[96,2048]{1,0:T(8,128)(2,1)S(1)} %pad_maximum_fusion), channel_id=1, source_target_pairs={{0,0},{1,64},{2,128},{3,192},{64,1},{65,65},{66,129},{67,193},{128... | collective-permute-start | bytes 1179656 | tf_op jit(solution)/shard_map/ppermute | solution.py:29
  53.3 36.1 %copy-start.20 = (bf16[96,2048]{1,0:T(8,128)(2,1)}, bf16[96,2048]{1,0:T(8,128)(2,1)S(1)}, u32[]{:S(2)}) copy-start(bf16[96,2048]{1,0:T(8,128)(2,1)S(1)} %collective-permute-done.5.near1) | copy-start | bytes 1179652
  53.3 3.3 %collective-permute-start.7 = (bf16[8,112,256]{2,1,0:T(8,128)(2,1)S(1)}, bf16[8,112,256]{2,1,0:T(8,128)(2,1)S(1)}, u32[]{:S(2)}, u32[]{:S(2)}) collective-permute-start(bf16[8,112,256]{2,1,0:T(8,128)(2,1)S(1)} %all-to-all-done.own0), channel_id=1, source_target_pairs={{0,64},{64,0},{1,65},{65,1},{2,66},{66,2},{3,67},{67,3},{4,68},{68... | collective-permute-start | bytes 1376264 | tf_op jit(solution)/shard_map/ppermute | solution.py:29
  53.7 3.6 %copy-start.15 = (bf16[8,112,256]{2,1,0:T(8,128)(2,1)}, bf16[8,112,256]{2,1,0:T(8,128)(2,1)S(1)}, u32[]{:S(2)}) copy-start(bf16[8,112,256]{2,1,0:T(8,128)(2,1)S(1)} %collective-permute-done.3.own2) | copy-start | bytes 1376260
  53.7 3.0 %collective-permute-start.9 = (bf16[8,112,256]{2,1,0:T(8,128)(2,1)S(1)}, bf16[8,112,256]{2,1,0:T(8,128)(2,1)S(1)}, u32[]{:S(2)}, u32[]{:S(2)}) collective-permute-start(bf16[8,112,256]{2,1,0:T(8,128)(2,1)S(1)} %collective-permute-done.3.own2), channel_id=1, source_target_pairs={{0,64},{64,0},{1,65},{65,1},{2,66},{66,2},{3,67},{67,3},{4,68},{68... | collective-permute-start | bytes 1376264 | tf_op jit(solution)/shard_map/ppermute | solution.py:29
  54.0 3.3 %copy-start.16 = (bf16[8,112,256]{2,1,0:T(8,128)(2,1)}, bf16[8,112,256]{2,1,0:T(8,128)(2,1)S(1)}, u32[]{:S(2)}) copy-start(bf16[8,112,256]{2,1,0:T(8,128)(2,1)S(1)} %collective-permute-done.6.own3) | copy-start | bytes 1376260
  54.0 2.7 %collective-permute-start.10 = (bf16[8,112,256]{2,1,0:T(8,128)(2,1)S(1)}, bf16[8,112,256]{2,1,0:T(8,128)(2,1)}, u32[]{:S(2)}, u32[]{:S(2)}) collective-permute-start(bf16[8,112,256]{2,1,0:T(8,128)(2,1)S(1)} %collective-permute-done.6.own3), channel_id=1, source_target_pairs={{0,64},{64,0},{1,65},{65,1},{2,66},{66,2},{3,67},{67,3},{4,68},{68... | collective-permute-start | bytes 1376264 | tf_op jit(solution)/shard_map/ppermute | solution.py:29
  54.3 3.0 %copy-start.17 = (bf16[8,112,256]{2,1,0:T(8,128)(2,1)}, bf16[8,112,256]{2,1,0:T(8,128)(2,1)S(1)}, u32[]{:S(2)}) copy-start(bf16[8,112,256]{2,1,0:T(8,128)(2,1)S(1)} %collective-permute-done.2.own1) | copy-start | bytes 1376260
  54.3 3.0 %collective-permute-start.8 = (bf16[8,112,256]{2,1,0:T(8,128)(2,1)S(1)}, bf16[8,112,256]{2,1,0:T(8,128)(2,1)}, u32[]{:S(2)}, u32[]{:S(2)}) collective-permute-start(bf16[8,112,256]{2,1,0:T(8,128)(2,1)S(1)} %collective-permute-done.2.own1), channel_id=1, source_target_pairs={{0,64},{64,0},{1,65},{65,1},{2,66},{66,2},{3,67},{67,3},{4,68},{68... | collective-permute-start | bytes 1376264 | tf_op jit(solution)/shard_map/ppermute | solution.py:29
  56.6 36.5 %copy-start.12 = (f32[96]{0:T(128)S(1)}, f32[96]{0:T(128)}, u32[]{:S(2)}) copy-start(f32[96]{0:T(128)} %param.21) | copy-start | bytes 1156
  56.6 37.2 %copy-start.13 = (f32[96]{0:T(128)S(1)}, f32[96]{0:T(128)}, u32[]{:S(2)}) copy-start(f32[96]{0:T(128)} %param.22) | copy-start | bytes 1156
  56.6 0.8 copy-start.18
  56.7 0.9 copy-start.19
  66.6 15.2 %collective-permute-start.11 = (bf16[96,256]{1,0:T(8,128)(2,1)}, bf16[96,256]{1,0:T(8,128)(2,1)S(1)}, u32[]{:S(2)}, u32[]{:S(2)}) collective-permute-start(bf16[96,256]{1,0:T(8,128)(2,1)} %get-tuple-element.32), channel_id=1, source_target_pairs={{0,0},{16,32},{32,64},{48,96},{64,16},{80,48},{96,80},{112,112},{1... | collective-permute-start | bytes 147464 | tf_op jit(solution)/shard_map/ppermute | solution.py:29
  69.4 12.4 %collective-permute-start.12 = (bf16[96,256]{1,0:T(8,128)(2,1)}, bf16[96,256]{1,0:T(8,128)(2,1)S(1)}, u32[]{:S(2)}, u32[]{:S(2)}) collective-permute-start(bf16[96,256]{1,0:T(8,128)(2,1)} %get-tuple-element.33), channel_id=1, source_target_pairs={{0,64},{16,96},{32,0},{48,32},{64,80},{80,112},{96,16},{112,48},{1... | collective-permute-start | bytes 147464 | tf_op jit(solution)/shard_map/ppermute | solution.py:29
  70.4 12.9 %collective-permute-start.13 = (bf16[96,256]{1,0:T(8,128)(2,1)}, bf16[96,256]{1,0:T(8,128)(2,1)S(1)}, u32[]{:S(2)}, u32[]{:S(2)}) collective-permute-start(bf16[96,256]{1,0:T(8,128)(2,1)} %get-tuple-element.34), channel_id=1, source_target_pairs={{0,128},{16,160},{32,192},{48,224},{64,144},{80,176},{96,208},{112... | collective-permute-start | bytes 147464 | tf_op jit(solution)/shard_map/ppermute | solution.py:29
  78.9 6.7 %collective-permute-start.14 = (bf16[96,256]{1,0:T(8,128)(2,1)}, bf16[96,256]{1,0:T(8,128)(2,1)S(1)}, u32[]{:S(2)}, u32[]{:S(2)}) collective-permute-start(bf16[96,256]{1,0:T(8,128)(2,1)} %get-tuple-element.35), channel_id=1, source_target_pairs={{0,192},{16,224},{32,128},{48,160},{64,208},{80,240},{96,144},{112... | collective-permute-start | bytes 147464 | tf_op jit(solution)/shard_map/ppermute | solution.py:29
  81.7 3.9 %copy-start.5 = (bf16[96,256]{1,0:T(8,128)(2,1)}, bf16[96,256]{1,0:T(8,128)(2,1)S(1)}, u32[]{:S(2)}) copy-start(bf16[96,256]{1,0:T(8,128)(2,1)S(1)} %collective-permute-done.11.piece0) | copy-start | bytes 147460
  81.7 3.9 %copy-start.6 = (bf16[96,256]{1,0:T(8,128)(2,1)}, bf16[96,256]{1,0:T(8,128)(2,1)S(1)}, u32[]{:S(2)}) copy-start(bf16[96,256]{1,0:T(8,128)(2,1)S(1)} %collective-permute-done.12.piece1) | copy-start | bytes 147460
  83.4 2.3 %copy-start.7 = (bf16[96,256]{1,0:T(8,128)(2,1)}, bf16[96,256]{1,0:T(8,128)(2,1)S(1)}, u32[]{:S(2)}) copy-start(bf16[96,256]{1,0:T(8,128)(2,1)S(1)} %collective-permute-done.13.piece2) | copy-start | bytes 147460
  85.7 0.6 copy-start.8
  88.0 24.0 %collective-permute-start.18 = (bf16[96,2048]{1,0:T(8,128)(2,1)}, bf16[96,2048]{1,0:T(8,128)(2,1)S(1)}, u32[]{:S(2)}, u32[]{:S(2)}) collective-permute-start(bf16[96,2048]{1,0:T(8,128)(2,1)} %collective-permute-done.4.near0), channel_id=1, source_target_pairs={{0,64},{64,0},{1,65},{65,1},{2,66},{66,2},{3,67},{67,3},{4,68},{68... | collective-permute-start | bytes 1179656 | tf_op jit(solution)/shard_map/ppermute | solution.py:29
  89.4 22.6 %collective-permute-start.19 = (bf16[96,2048]{1,0:T(8,128)(2,1)S(1)}, bf16[96,2048]{1,0:T(8,128)(2,1)S(1)}, u32[]{:S(2)}, u32[]{:S(2)}) collective-permute-start(bf16[96,2048]{1,0:T(8,128)(2,1)S(1)} %collective-permute-done.5.near1), channel_id=1, source_target_pairs={{0,64},{64,0},{1,65},{65,1},{2,66},{66,2},{3,67},{67,3},{4,68},{68... | collective-permute-start | bytes 1179656 | tf_op jit(solution)/shard_map/ppermute | solution.py:29
  89.5 22.5 %collective-permute-start.17 = (bf16[96,1024]{1,0:T(8,128)(2,1)}, bf16[96,1024]{1,0:T(8,128)(2,1)S(1)}, u32[]{:S(2)}, u32[]{:S(2)}) collective-permute-start(bf16[96,1024]{1,0:T(8,128)(2,1)} %get-tuple-element.36.clip0.clip), channel_id=1, source_target_pairs={{0,3},{1,0},{2,1},{3,2},{4,7},{5,4},{6,5},{7,6},{8,11},{9,8},{10,9... | collective-permute-start | bytes 589832 | tf_op jit(solution)/shard_map/ppermute | solution.py:29
  91.0 21.0 %collective-permute-start.16 = (bf16[96,1024]{1,0:T(8,128)(2,1)}, bf16[96,1024]{1,0:T(8,128)(2,1)S(1)}, u32[]{:S(2)}, u32[]{:S(2)}) collective-permute-start(bf16[96,1024]{1,0:T(8,128)(2,1)} %get-tuple-element.36.clip0.clip), channel_id=1, source_target_pairs={{0,2},{1,3},{2,0},{3,1},{4,6},{5,7},{6,4},{7,5},{8,10},{9,11},{10,... | collective-permute-start | bytes 589832 | tf_op jit(solution)/shard_map/ppermute | solution.py:29
  92.3 19.7 %collective-permute-start.15 = (bf16[96,1024]{1,0:T(8,128)(2,1)}, bf16[96,1024]{1,0:T(8,128)(2,1)S(1)}, u32[]{:S(2)}, u32[]{:S(2)}) collective-permute-start(bf16[96,1024]{1,0:T(8,128)(2,1)} %get-tuple-element.36.clip0.clip), channel_id=1, source_target_pairs={{0,1},{1,2},{2,3},{3,0},{4,5},{5,6},{6,7},{7,4},{8,9},{9,10},{10,1... | collective-permute-start | bytes 589832 | tf_op jit(solution)/shard_map/ppermute | solution.py:29
  94.6 17.4 %all-to-all-start.1 = ((f32[64,1,128]{2,1,0:T(1,128)}), f32[64,1,128]{2,1,0:T(1,128)S(1)}, u32[]{:S(2)}, u32[]{:S(2)}) async-start(f32[64,1,128]{2,1,0:T(1,128)} %get-tuple-element.37), calls=%async_computation.1 | async-start | bytes 65536 | tf_op jit(solution)/shard_map/all_to_all | solution.py:447
  112.0 0.6 copy-start.9
  112.0 0.7 copy-start.23
  112.0 0.8 copy-start.24
  112.0 0.8 copy-start.25
  112.0 0.9 copy-start.21
  112.0 1.0 copy-start.22
  113.1 18.3 %copy-start.1 = (bf16[3,3,3,96,384]{4,3,2,1,0:T(8,128)(2,1)S(1)}, bf16[3,3,3,96,384]{4,3,2,1,0:T(8,128)(2,1)}, u32[]{:S(2)}) copy-start(bf16[3,3,3,96,384]{4,3,2,1,0:T(8,128)(2,1)} %param.23) | copy-start | bytes 5971972
  119.6 14.2 %collective-permute-start.20 = (bf16[96,512]{1,0:T(8,128)(2,1)}, bf16[96,512]{1,0:T(8,128)(2,1)S(1)}, u32[]{:S(2)}, u32[]{:S(2)}) collective-permute-start(bf16[96,512]{1,0:T(8,128)(2,1)} %get-tuple-element.45), channel_id=1, source_target_pairs={{0,4},{4,8},{8,12},{12,16},{16,20},{20,24},{24,28},{28,32},{32,36}... | collective-permute-start | bytes 294920 | tf_op jit(solution)/shard_map/ppermute | solution.py:29
  121.8 12.0 %collective-permute-start.21 = (bf16[96,512]{1,0:T(8,128)(2,1)}, bf16[96,512]{1,0:T(8,128)(2,1)S(1)}, u32[]{:S(2)}, u32[]{:S(2)}) collective-permute-start(bf16[96,512]{1,0:T(8,128)(2,1)} %get-tuple-element.46), channel_id=1, source_target_pairs={{4,0},{8,4},{12,8},{16,12},{20,16},{24,20},{28,24},{32,28},{36,32}... | collective-permute-start | bytes 294920 | tf_op jit(solution)/shard_map/ppermute | solution.py:29
  127.6 19.9 %all-to-all-start.2 = ((bf16[16,8,16,128]{3,2,1,0:T(8,128)(2,1)}), bf16[16,8,16,128]{3,2,1,0:T(8,128)(2,1)S(1)}, u32[]{:S(2)}, u32[]{:S(2)}) async-start(bf16[16,8,16,128]{3,2,1,0:T(8,128)(2,1)} %bitcast.45), calls=%async_computation.2 | async-start | bytes 1048576 | tf_op jit(solution)/shard_map/all_to_all | solution.py:470
  133.7 0.6 copy-start.26
  134.4 0.6 copy-start.27
  140.9 5.3 %collective-permute-start.22 = (bf16[2,96,1024]{2,1,0:T(8,128)(2,1)}, bf16[2,96,1024]{2,1,0:T(8,128)(2,1)S(1)}, u32[]{:S(2)}, u32[]{:S(2)}) collective-permute-start(bf16[2,96,1024]{2,1,0:T(8,128)(2,1)} %get-tuple-element.49), channel_id=1, source_target_pairs={{0,64},{64,0},{1,65},{65,1},{2,66},{66,2},{3,67},{67,3},{4,68},{68... | collective-permute-start | bytes 1179656 | tf_op jit(solution)/shard_map/ppermute | solution.py:29
  170.6 18.0 %copy-start.4 = (bf16[96,1024]{1,0:T(8,128)(2,1)S(1)}, bf16[96,1024]{1,0:T(8,128)(2,1)}, u32[]{:S(2)}) copy-start(bf16[96,1024]{1,0:T(8,128)(2,1)} %get-tuple-element.36.clip0.clip) | copy-start | bytes 589828
  170.6 18.0 %copy-start.14 = (f32[96]{0:T(128)S(1)}, f32[96]{0:T(128)}, u32[]{:S(2)}) copy-start(f32[96]{0:T(128)} %param.24) | copy-start | bytes 1156
  170.6 28.9 %all-to-all-start.4 = ((bf16[4,128,16,128]{3,2,1,0:T(8,128)(2,1)}), bf16[4,128,16,128]{3,2,1,0:T(8,128)(2,1)S(1)}, u32[]{:S(2)}, u32[]{:S(2)}) async-start(bf16[4,128,16,128]{3,2,1,0:T(8,128)(2,1)} %broadcast_in_dim.40), calls=%async_computation.4 | async-start | bytes 4194304 | tf_op jit(solution)/shard_map/all_to_all | solution.py:50
  174.3 14.3 %collective-permute-start.23 = (bf16[96,1024]{1,0:T(8,128)(2,1)S(1)}, bf16[96,1024]{1,0:T(8,128)(2,1)S(1)}, u32[]{:S(2)}, u32[]{:S(2)}) collective-permute-start(bf16[96,1024]{1,0:T(8,128)(2,1)S(1)} %fusion.1), channel_id=1, source_target_pairs={{0,128},{128,0},{1,129},{129,1},{2,130},{130,2},{3,131},{131,3},{4... | collective-permute-start | bytes 589832 | tf_op jit(solution)/shard_map/ppermute | solution.py:29
  199.5 1.3 copy-start

commit v2 on v0

--- a/solution.py
+++ b/solution.py
@@ -451,6 +451,8 @@
     packed = packed.reshape(16, 4, 1, 128)
     gain, shift = norm2_gain[:, None], norm2_shift[:, None]
 
+    above, below = halo(last, leading)
+    clips, above, below = lax.optimization_barrier((clips, above, below))
     table = pl.pallas_call(
         grad_kernel,
         out_shape=jax.ShapeDtypeStruct((128, 16, 128), BF),
@@ -467,8 +469,7 @@
         cost_estimate=cost(4 * 10**9, 20 * 10**6),
         name="weight_grad",
     )(jnp.stack([y, co, zh]).astype(jnp.int32), packed, *clips, *near, *far, gain, shift)
-    table, conv_weight, last, leading = lax.optimization_barrier((table, conv_weight, last, leading))
-    above, below = halo(last, leading)
+    table, conv_weight = lax.optimization_barrier((table, conv_weight))
     kernels = conv_weight.transpose(0, 4, 1, 2, 3).reshape(3, 384, 864)
     shares = lax.all_to_all(table.reshape(16, 8, 16, 128), ("zl", "x"), 0, 0, tiled=True)
     keep, send = pl.pallas_call(

time: 206 us -> 204 us (level)
  no operation moved by 1% of the time
where the time goes in v2:
time: 204 us; the launch traced here: 203 us
  starting transfers between devices  76.8 us (38%)
  waiting for transfers between devices  56.6 us (28%)
  Pallas kernels  29.3 us (14%)
  blocking collectives  21.4 us (10%)
  local copies, waits for them, and re-layouts  11.9 us (6%)
  other arithmetic  4.93 us (2%)
    ppermute x27, starting transfers between devices, permute(): return lax.ppermute(value, axes, pairs)  54.1 us
    ppermute x27, waiting for transfers between devices, permute(): return lax.ppermute(value, axes, pairs)  50.3 us
    all_to_all x1, blocking collectives, spread(): return lax.all_to_all(copies, axes, 0, 0, tiled=True)  21.4 us
    all_to_all x1, starting transfers between devices, body(): packed = lax.all_to_all(packed, ('zl', 'x', 'y'), 0, 0, tiled=True)  9.28 us
    pallas_call x1, Pallas kernels, body(): pl.pallas_call(attend_kernel, out_shape=[jax.ShapeDtypeStruct((96, 256),...  9 us
    all_to_all x1, starting transfers between devices, body(): mine = lax.all_to_all(by_frame, ('zh', 'zl'), 0, 0, tiled=True)  7.69 us
    pallas_call x1, Pallas kernels, body(): pl.pallas_call(grad_kernel, out_shape=jax.ShapeDtypeStruct((128, 16, 128)...  6.52 us
    all_to_all x1, waiting for transfers between devices, body(): packed = lax.all_to_all(packed, ('zl', 'x', 'y'), 0, 0, tiled=True)  6.3 us
  transfers between devices with their start and end apart: 30, of which 12 were waited for; matrix products, arithmetic and copies ran while one was open for 6% of the time, Pallas kernels for 3%

profile of v2, /device:TPU:65, one launch (start us, length us, event | category | flops | bytes accessed | tf_op | source)
XLA Modules:
  0.0 202.6 jit_solution(6180514441018492220)
XLA Ops:
  1.3 1.7 reshape.59.frames
  3.0 1.9 pack.1
  4.9 7.7 %all-to-all-start = ((bf16[8,112,256]{2,1,0:T(8,128)(2,1)}), bf16[8,112,256]{2,1,0:T(8,128)(2,1)S(1)}, u32[]{:S(2)}, u32[]{:S(2)}) async-start(bf16[8,112,256]{2,1,0:T(8,128)(2,1)} %pack.1), calls=%async_computation | async-start | bytes 917504 | tf_op jit(solution)/shard_map/all_to_all | solution.py:379
  12.6 0.2 bitcast_multiply_fusion.1
  12.9 1.1 slice_reduce_fusion.1
  14.0 4.4 %collective-permute-start.1 = (bf16[96,512]{1,0:T(8,128)(2,1)S(1)}, bf16[96,512]{1,0:T(8,128)(2,1)S(1)}, u32[]{:S(2)}, u32[]{:S(2)}) collective-permute-start(bf16[96,512]{1,0:T(8,128)(2,1)S(1)} %bitcast.51), channel_id=1, source_target_pairs={{4,0},{8,4},{12,8},{16,12},{20,16},{24,20},{28,24},{32,28},{36,32}... | collective-permute-start | bytes 294920 | tf_op jit(solution)/shard_map/ppermute | solution.py:29
  18.4 1.9 collective-permute-start
  20.6 2.2 %collective-permute-done.1 = bf16[96,512]{1,0:T(8,128)(2,1)S(1)} collective-permute-done((bf16[96,512]{1,0:T(8,128)(2,1)S(1)}, bf16[96,512]{1,0:T(8,128)(2,1)S(1)}, u32[]{:S(2)}, u32[]{:S(2)}) %collective-permute-start.1) | collective-permute-done | bytes 98336 | tf_op jit(solution)/shard_map/ppermute | solution.py:29
  22.8 3.6 %collective-permute-done = bf16[96,512]{1,0:T(8,128)(2,1)S(1)} collective-permute-done((bf16[96,512]{1,0:T(8,128)(2,1)S(1)}, bf16[96,512]{1,0:T(8,128)(2,1)S(1)}, u32[]{:S(2)}, u32[]{:S(2)}) %collective-permute-start) | collective-permute-done | bytes 98336 | tf_op jit(solution)/shard_map/ppermute | solution.py:29
  26.5 0.7 collective-permute-start.3
  27.2 1.3 collective-permute-start.6
  28.5 0.5 collective-permute-start.2
  29.0 8.0 %collective-permute-start.5 = (bf16[96,2048]{1,0:T(8,128)(2,1)S(1)}, bf16[96,2048]{1,0:T(8,128)(2,1)}, u32[]{:S(2)}, u32[]{:S(2)}) collective-permute-start(bf16[96,2048]{1,0:T(8,128)(2,1)S(1)} %pad_maximum_fusion), channel_id=1, source_target_pairs={{0,128},{1,192},{2,0},{3,64},{64,129},{65,193},{66,1},{67,65},{128... | collective-permute-start | bytes 1179656 | tf_op jit(solution)/shard_map/ppermute | solution.py:29
  37.0 1.9 collective-permute-start.4
  38.9 14.4 %collective-permute-done.5.near1 = bf16[96,2048]{1,0:T(8,128)(2,1)} collective-permute-done((bf16[96,2048]{1,0:T(8,128)(2,1)S(1)}, bf16[96,2048]{1,0:T(8,128)(2,1)}, u32[]{:S(2)}, u32[]{:S(2)}) %collective-permute-start.5) | collective-permute-done | bytes 393248 | tf_op jit(solution)/shard_map/ppermute | solution.py:29
  53.3 0.3 collective-permute-start.7
  53.7 0.3 collective-permute-start.9
  54.0 0.3 collective-permute-start.10
  54.3 0.3 collective-permute-start.8
  54.6 0.6 broadcast_in_dim.30.qkv_bias
  55.2 0.8 broadcast_in_dim.35.out_bias
  56.0 0.7 pad_add_fusion.1.at
  56.6 0.5 collective-permute-done.10.other3
  57.4 0.5 copy-done.23
  58.1 9.0 %attention.1 = (bf16[96,256]{1,0:T(8,128)(2,1)}, bf16[96,256]{1,0:T(8,128)(2,1)}, bf16[96,256]{1,0:T(8,128)(2,1)}, bf16[96,256]{1,0:T(8,128)(2,1)}) custom-call(s32[4]{0:T(128)} %pad_add_fusion.1.at, bf16[8,112,256]{2,1,0:T(8,128)(2,1)} %copy-done.6, bf16[8,112,256]{2,1,0:T(8,128)(2,1)} %copy-done.20, bf16[8,112,256]{2,1,0:T(8,128)(2,1)} %copy-done.18, ...), custom_call_target="tpu_custom_call" | custom-call | flops 4000000000 | bytes 20000000 | tf_op jit(solution)/shard_map/attention/pallas_call | solution.py:399
  67.1 2.9 %collective-permute-start.11 = (bf16[96,256]{1,0:T(8,128)(2,1)}, bf16[96,256]{1,0:T(8,128)(2,1)S(1)}, u32[]{:S(2)}, u32[]{:S(2)}) collective-permute-start(bf16[96,256]{1,0:T(8,128)(2,1)} %get-tuple-element.36), channel_id=1, source_target_pairs={{0,0},{16,32},{32,64},{48,96},{64,16},{80,48},{96,80},{112,112},{1... | collective-permute-start | bytes 147464 | tf_op jit(solution)/shard_map/ppermute | solution.py:29
  69.9 1.0 collective-permute-start.12
  71.0 8.1 %collective-permute-start.13 = (bf16[96,256]{1,0:T(8,128)(2,1)}, bf16[96,256]{1,0:T(8,128)(2,1)S(1)}, u32[]{:S(2)}, u32[]{:S(2)}) collective-permute-start(bf16[96,256]{1,0:T(8,128)(2,1)} %get-tuple-element.38), channel_id=1, source_target_pairs={{0,128},{16,160},{32,192},{48,224},{64,144},{80,176},{96,208},{112... | collective-permute-start | bytes 147464 | tf_op jit(solution)/shard_map/ppermute | solution.py:29
  79.1 2.3 %collective-permute-start.14 = (bf16[96,256]{1,0:T(8,128)(2,1)}, bf16[96,256]{1,0:T(8,128)(2,1)S(1)}, u32[]{:S(2)}, u32[]{:S(2)}) collective-permute-start(bf16[96,256]{1,0:T(8,128)(2,1)} %get-tuple-element.39), channel_id=1, source_target_pairs={{0,192},{16,224},{32,128},{48,160},{64,208},{80,240},{96,144},{112... | collective-permute-start | bytes 147464 | tf_op jit(solution)/shard_map/ppermute | solution.py:29
  81.4 0.6 pad_add_fusion.at
  82.0 1.6 collective-permute-done.13.piece2
  83.6 2.2 %collective-permute-done.14.piece3 = bf16[96,256]{1,0:T(8,128)(2,1)S(1)} collective-permute-done((bf16[96,256]{1,0:T(8,128)(2,1)}, bf16[96,256]{1,0:T(8,128)(2,1)S(1)}, u32[]{:S(2)}, u32[]{:S(2)}) %collective-permute-start.14) | collective-permute-done | bytes 49184 | tf_op jit(solution)/shard_map/ppermute | solution.py:29
  85.8 0.6 copy-done.11
  86.4 1.7 arrange.1
  88.1 1.5 collective-permute-start.20
  89.7 3.6 %collective-permute-start.18 = (bf16[96,512]{1,0:T(8,128)(2,1)}, bf16[96,512]{1,0:T(8,128)(2,1)S(1)}, u32[]{:S(2)}, u32[]{:S(2)}) collective-permute-start(bf16[96,512]{1,0:T(8,128)(2,1)} %get-tuple-element.42), channel_id=1, source_target_pairs={{0,4},{4,8},{8,12},{12,16},{16,20},{20,24},{24,28},{28,32},{32,36}... | collective-permute-start | bytes 294920 | tf_op jit(solution)/shard_map/ppermute | solution.py:29
  93.3 3.8 %collective-permute-start.19 = (bf16[96,512]{1,0:T(8,128)(2,1)}, bf16[96,512]{1,0:T(8,128)(2,1)S(1)}, u32[]{:S(2)}, u32[]{:S(2)}) collective-permute-start(bf16[96,512]{1,0:T(8,128)(2,1)} %get-tuple-element.43), channel_id=1, source_target_pairs={{4,0},{8,4},{12,8},{16,12},{20,16},{24,20},{28,24},{32,28},{36,32}... | collective-permute-start | bytes 294920 | tf_op jit(solution)/shard_map/ppermute | solution.py:29
  97.1 0.7 copy.22.gain
  97.8 0.7 copy.23.shift
  98.5 1.5 collective-permute-start.17
  100.1 1.3 collective-permute-start.16
  101.4 0.8 collective-permute-start.15
  102.1 0.6 pad_add_fusion.3.at
  102.8 9.3 %all-to-all-start.1 = ((f32[64,1,128]{2,1,0:T(1,128)}), f32[64,1,128]{2,1,0:T(1,128)S(1)}, u32[]{:S(2)}, u32[]{:S(2)}) async-start(f32[64,1,128]{2,1,0:T(1,128)} %get-tuple-element.41), calls=%async_computation.1 | async-start | bytes 65536 | tf_op jit(solution)/shard_map/all_to_all | solution.py:450
  112.1 0.6 pad_add_fusion.2.at
  112.8 6.3 %all-to-all-done.1 = f32[64,1,128]{2,1,0:T(1,128)S(1)} async-done(((f32[64,1,128]{2,1,0:T(1,128)}), f32[64,1,128]{2,1,0:T(1,128)S(1)}, u32[]{:S(2)}, u32[]{:S(2)}) %all-to-all-start.1) | async-done | bytes 32800 | tf_op jit(solution)/shard_map/all_to_all | solution.py:450
  119.2 0.5 copy-done.12
  120.0 6.5 %weight_grad.1 = bf16[128,16,128]{2,1,0:T(8,128)(2,1)} custom-call(s32[3]{0:T(128)} %pad_add_fusion.2.at, f32[16,4,1,128]{3,2,1,0:T(1,128)} %bitcast.53, bf16[96,1024]{1,0:T(8,128)(2,1)} %get-tuple-element.44.clip0.clip, bf16[96,1024]{1,0:T(8,128)(2,1)} %copy-done.28, bf16[96,1024]{1,0:T(8,128)(2,1)} %copy-done.27, bf16[96,1024]{1,0:T(8,128)(2,1)} %copy-done.26, ...), custom_call_target="tpu_custom_call" | custom-call | flops 4000000000 | bytes 20000000 | tf_op jit(solution)/shard_map/weight_grad/pallas_call | solution.py:456
  126.5 5.7 %all-to-all-start.2 = ((bf16[16,8,16,128]{3,2,1,0:T(8,128)(2,1)}), bf16[16,8,16,128]{3,2,1,0:T(8,128)(2,1)S(1)}, u32[]{:S(2)}, u32[]{:S(2)}) async-start(bf16[16,8,16,128]{3,2,1,0:T(8,128)(2,1)} %bitcast.48), calls=%async_computation.2 | async-start | bytes 1048576 | tf_op jit(solution)/shard_map/all_to_all | solution.py:474
  132.2 2.4 %copy.24.weight = bf16[3,384,864]{2,1,0:T(8,128)(2,1)} copy(bf16[3,384,864]{1,2,0:T(8,128)(2,1)S(1)} %bitcast.47) | data formatting | bytes 3981312 | tf_op jit(solution)/shard_map/reshape | solution.py:473
  134.6 5.8 %convolution.1 = (bf16[2,96,1024]{2,1,0:T(8,128)(2,1)}, bf16[2,96,1024]{2,1,0:T(8,128)(2,1)}) custom-call(s32[3]{0:T(128)} %pad_add_fusion.3.at, f32[16,4,1,128]{3,2,1,0:T(1,128)} %bitcast.54, bf16[96,1024]{1,0:T(8,128)(2,1)} %get-tuple-element.44.clip0.clip, bf16[96,512]{1,0:T(8,128)(2,1)} %copy-done.29, bf16[96,512]{1,0:T(8,128)(2,1)} %copy-done.30, ...), custom_call_target="tpu_custom_call" | custom-call | flops 3000000000 | bytes 12000000 | tf_op jit(solution)/shard_map/convolution/pallas_call | solution.py:475
  140.5 3.9 %collective-permute-start.22 = (bf16[2,96,1024]{2,1,0:T(8,128)(2,1)}, bf16[2,96,1024]{2,1,0:T(8,128)(2,1)S(1)}, u32[]{:S(2)}, u32[]{:S(2)}) collective-permute-start(bf16[2,96,1024]{2,1,0:T(8,128)(2,1)} %get-tuple-element.57), channel_id=1, source_target_pairs={{0,64},{64,0},{1,65},{65,1},{2,66},{66,2},{3,67},{67,3},{4,68},{68... | collective-permute-start | bytes 1179656 | tf_op jit(solution)/shard_map/ppermute | solution.py:29
  144.4 1.6 collective-permute-done.22
  145.9 1.1 convert_add_fusion
  147.3 21.4 %all_to_all.20 = bf16[16,8,16,128]{3,2,1,0:T(8,128)(2,1)S(1)} all-to-all(bf16[16,8,16,128]{3,2,1,0:T(8,128)(2,1)S(1)} %broadcast_in_dim.34), channel_id=1, replica_groups=mesh['zh'=2,'co'=2,'zl'=4,'x'=4,'y'=4] {'zl','x'}, dimensions={0} | all-to-all | bytes 1048576 | tf_op jit(solution)/shard_map/all_to_all | solution.py:50
  168.7 1.4 collective-permute-start.23
  170.2 0.6 collective-permute-start.26
  170.8 1.4 collective-permute-start.25
  172.2 10.7 %collective-permute-done.23 = bf16[96,1024]{1,0:T(8,128)(2,1)S(1)} collective-permute-done((bf16[96,1024]{1,0:T(8,128)(2,1)S(1)}, bf16[96,1024]{1,0:T(8,128)(2,1)S(1)}, u32[]{:S(2)}, u32[]{:S(2)}) %collective-permute-start.23) | collective-permute-done | bytes 196640 | tf_op jit(solution)/shard_map/ppermute | solution.py:29
  183.0 0.3 reshape.66
  183.4 0.9 fusion
  184.3 13.1 %collective-permute-done.24.table1 = bf16[128,16,128]{2,1,0:T(8,128)(2,1)S(1)} collective-permute-done((bf16[128,16,128]{2,1,0:T(8,128)(2,1)S(1)}, bf16[128,16,128]{2,1,0:T(8,128)(2,1)S(1)}, u32[]{:S(2)}, u32[]{:S(2)}) %collective-permute-start.24) | collective-permute-done | bytes 524320 | tf_op jit(solution)/shard_map/ppermute | solution.py:29
  197.4 0.8 copy-done.5
  198.2 4.4 %join.1 = f32[2592,384]{1,0:T(8,128)} custom-call(s32[1]{0:T(128)} %bitcast.8.at, bf16[128,16,128]{2,1,0:T(8,128)(2,1)} %bitcast.46, bf16[128,16,128]{2,1,0:T(8,128)(2,1)} %copy-done.5, bf16[128,16,128]{2,1,0:T(8,128)(2,1)} %copy-done.4, bf16[128,16,128]{2,1,0:T(8,128)(2,1)} %copy-done.3), custom_call_target="tpu_custom_call" | custom-call | flops 1000000 | bytes 6000000 | tf_op jit(solution)/shard_map/join/pallas_call | solution.py:502
  (94 shorter events, 1.7 us)
Async XLA Ops:
  0.6 12.0 %copy-start.2 = (bf16[96,1,4,2,128]{4,3,2,1,0:T(2,128)(2,1)S(1)}, bf16[96,1,4,2,128]{4,3,2,1,0:T(2,128)(2,1)}, u32[]{:S(2)}) copy-start(bf16[96,1,4,2,128]{4,3,2,1,0:T(2,128)(2,1)} %param.25) | copy-start | bytes 589828
  4.9 49.7 %copy-start.13 = (f32[1152]{0:T(1024)S(1)}, f32[1152]{0:T(1024)}, u32[]{:S(2)}) copy-start(f32[1152]{0:T(1024)} %param.18) | copy-start | bytes 13828
  4.9 50.2 %copy-start.14 = (f32[384]{0:T(512)S(1)}, f32[384]{0:T(512)}, u32[]{:S(2)}) copy-start(f32[384]{0:T(512)} %param.20) | copy-start | bytes 4612
  4.9 21.5 %all-to-all-start = ((bf16[8,112,256]{2,1,0:T(8,128)(2,1)}), bf16[8,112,256]{2,1,0:T(8,128)(2,1)S(1)}, u32[]{:S(2)}, u32[]{:S(2)}) async-start(bf16[8,112,256]{2,1,0:T(8,128)(2,1)} %pack.1), calls=%async_computation | async-start | bytes 917504 | tf_op jit(solution)/shard_map/all_to_all | solution.py:379
  14.0 8.8 %collective-permute-start.1 = (bf16[96,512]{1,0:T(8,128)(2,1)S(1)}, bf16[96,512]{1,0:T(8,128)(2,1)S(1)}, u32[]{:S(2)}, u32[]{:S(2)}) collective-permute-start(bf16[96,512]{1,0:T(8,128)(2,1)S(1)} %bitcast.51), channel_id=1, source_target_pairs={{4,0},{8,4},{12,8},{16,12},{20,16},{24,20},{28,24},{32,28},{36,32}... | collective-permute-start | bytes 294920 | tf_op jit(solution)/shard_map/ppermute | solution.py:29
  18.4 8.0 %collective-permute-start = (bf16[96,512]{1,0:T(8,128)(2,1)S(1)}, bf16[96,512]{1,0:T(8,128)(2,1)S(1)}, u32[]{:S(2)}, u32[]{:S(2)}) collective-permute-start(bf16[96,512]{1,0:T(8,128)(2,1)S(1)} %bitcast.52), channel_id=1, source_target_pairs={{0,4},{4,8},{8,12},{12,16},{16,20},{20,24},{24,28},{28,32},{32,36}... | collective-permute-start | bytes 294920 | tf_op jit(solution)/shard_map/ppermute | solution.py:29
  26.5 30.8 %copy-start.6 = (bf16[8,112,256]{2,1,0:T(8,128)(2,1)}, bf16[8,112,256]{2,1,0:T(8,128)(2,1)S(1)}, u32[]{:S(2)}) copy-start(bf16[8,112,256]{2,1,0:T(8,128)(2,1)S(1)} %all-to-all-done.own0) | copy-start | bytes 1376260
  26.5 27.2 %collective-permute-start.3 = (bf16[8,112,256]{2,1,0:T(8,128)(2,1)S(1)}, bf16[8,112,256]{2,1,0:T(8,128)(2,1)S(1)}, u32[]{:S(2)}, u32[]{:S(2)}) collective-permute-start(bf16[8,112,256]{2,1,0:T(8,128)(2,1)S(1)} %all-to-all-done.own0), channel_id=1, source_target_pairs={{0,8},{4,12},{8,0},{12,4},{1,9},{5,13},{9,1},{13,5},{2,10},{6,14},... | collective-permute-start | bytes 1376264 | tf_op jit(solution)/shard_map/ppermute | solution.py:29
  27.2 26.7 %collective-permute-start.6 = (bf16[8,112,256]{2,1,0:T(8,128)(2,1)S(1)}, bf16[8,112,256]{2,1,0:T(8,128)(2,1)S(1)}, u32[]{:S(2)}, u32[]{:S(2)}) collective-permute-start(bf16[8,112,256]{2,1,0:T(8,128)(2,1)S(1)} %all-to-all-done.own0), channel_id=1, source_target_pairs={{0,12},{4,0},{8,4},{12,8},{1,13},{5,1},{9,5},{13,9},{2,14},{6,2},{... | collective-permute-start | bytes 1376264 | tf_op jit(solution)/shard_map/ppermute | solution.py:29
  28.5 25.8 %collective-permute-start.2 = (bf16[8,112,256]{2,1,0:T(8,128)(2,1)S(1)}, bf16[8,112,256]{2,1,0:T(8,128)(2,1)S(1)}, u32[]{:S(2)}, u32[]{:S(2)}) collective-permute-start(bf16[8,112,256]{2,1,0:T(8,128)(2,1)S(1)} %all-to-all-done.own0), channel_id=1, source_target_pairs={{0,4},{4,8},{8,12},{12,0},{1,5},{5,9},{9,13},{13,1},{2,6},{6,10},{... | collective-permute-start | bytes 1376264 | tf_op jit(solution)/shard_map/ppermute | solution.py:29
  29.0 24.3 %collective-permute-start.5 = (bf16[96,2048]{1,0:T(8,128)(2,1)S(1)}, bf16[96,2048]{1,0:T(8,128)(2,1)}, u32[]{:S(2)}, u32[]{:S(2)}) collective-permute-start(bf16[96,2048]{1,0:T(8,128)(2,1)S(1)} %pad_maximum_fusion), channel_id=1, source_target_pairs={{0,128},{1,192},{2,0},{3,64},{64,129},{65,193},{66,1},{67,65},{128... | collective-permute-start | bytes 1179656 | tf_op jit(solution)/shard_map/ppermute | solution.py:29
  37.0 16.7 %collective-permute-start.4 = (bf16[96,2048]{1,0:T(8,128)(2,1)S(1)}, bf16[96,2048]{1,0:T(8,128)(2,1)}, u32[]{:S(2)}, u32[]{:S(2)}) collective-permute-start(bf16[96,2048]{1,0:T(8,128)(2,1)S(1)} %pad_maximum_fusion), channel_id=1, source_target_pairs={{0,0},{1,64},{2,128},{3,192},{64,1},{65,65},{66,129},{67,193},{128... | collective-permute-start | bytes 1179656 | tf_op jit(solution)/shard_map/ppermute | solution.py:29
  53.3 3.3 %collective-permute-start.7 = (bf16[8,112,256]{2,1,0:T(8,128)(2,1)S(1)}, bf16[8,112,256]{2,1,0:T(8,128)(2,1)S(1)}, u32[]{:S(2)}, u32[]{:S(2)}) collective-permute-start(bf16[8,112,256]{2,1,0:T(8,128)(2,1)S(1)} %all-to-all-done.own0), channel_id=1, source_target_pairs={{0,64},{64,0},{1,65},{65,1},{2,66},{66,2},{3,67},{67,3},{4,68},{68... | collective-permute-start | bytes 1376264 | tf_op jit(solution)/shard_map/ppermute | solution.py:29
  53.7 3.6 %copy-start.18 = (bf16[8,112,256]{2,1,0:T(8,128)(2,1)}, bf16[8,112,256]{2,1,0:T(8,128)(2,1)S(1)}, u32[]{:S(2)}) copy-start(bf16[8,112,256]{2,1,0:T(8,128)(2,1)S(1)} %collective-permute-done.3.own2) | copy-start | bytes 1376260
  53.7 3.5 %collective-permute-start.9 = (bf16[8,112,256]{2,1,0:T(8,128)(2,1)S(1)}, bf16[8,112,256]{2,1,0:T(8,128)(2,1)S(1)}, u32[]{:S(2)}, u32[]{:S(2)}) collective-permute-start(bf16[8,112,256]{2,1,0:T(8,128)(2,1)S(1)} %collective-permute-done.3.own2), channel_id=1, source_target_pairs={{0,64},{64,0},{1,65},{65,1},{2,66},{66,2},{3,67},{67,3},{4,68},{68... | collective-permute-start | bytes 1376264 | tf_op jit(solution)/shard_map/ppermute | solution.py:29
  54.0 3.3 %copy-start.19 = (bf16[8,112,256]{2,1,0:T(8,128)(2,1)}, bf16[8,112,256]{2,1,0:T(8,128)(2,1)S(1)}, u32[]{:S(2)}) copy-start(bf16[8,112,256]{2,1,0:T(8,128)(2,1)S(1)} %collective-permute-done.6.own3) | copy-start | bytes 1376260
  54.0 3.2 %collective-permute-start.10 = (bf16[8,112,256]{2,1,0:T(8,128)(2,1)S(1)}, bf16[8,112,256]{2,1,0:T(8,128)(2,1)S(1)}, u32[]{:S(2)}, u32[]{:S(2)}) collective-permute-start(bf16[8,112,256]{2,1,0:T(8,128)(2,1)S(1)} %collective-permute-done.6.own3), channel_id=1, source_target_pairs={{0,64},{64,0},{1,65},{65,1},{2,66},{66,2},{3,67},{67,3},{4,68},{68... | collective-permute-start | bytes 1376264 | tf_op jit(solution)/shard_map/ppermute | solution.py:29
  54.3 3.0 %copy-start.20 = (bf16[8,112,256]{2,1,0:T(8,128)(2,1)}, bf16[8,112,256]{2,1,0:T(8,128)(2,1)S(1)}, u32[]{:S(2)}) copy-start(bf16[8,112,256]{2,1,0:T(8,128)(2,1)S(1)} %collective-permute-done.2.own1) | copy-start | bytes 1376260
  54.3 3.0 %collective-permute-start.8 = (bf16[8,112,256]{2,1,0:T(8,128)(2,1)S(1)}, bf16[8,112,256]{2,1,0:T(8,128)(2,1)}, u32[]{:S(2)}, u32[]{:S(2)}) collective-permute-start(bf16[8,112,256]{2,1,0:T(8,128)(2,1)S(1)} %collective-permute-done.2.own1), channel_id=1, source_target_pairs={{0,64},{64,0},{1,65},{65,1},{2,66},{66,2},{3,67},{67,3},{4,68},{68... | collective-permute-start | bytes 1376264 | tf_op jit(solution)/shard_map/ppermute | solution.py:29
  56.6 40.5 %copy-start.15 = (f32[96]{0:T(128)S(1)}, f32[96]{0:T(128)}, u32[]{:S(2)}) copy-start(f32[96]{0:T(128)} %param.21) | copy-start | bytes 1156
  56.6 41.2 %copy-start.16 = (f32[96]{0:T(128)S(1)}, f32[96]{0:T(128)}, u32[]{:S(2)}) copy-start(f32[96]{0:T(128)} %param.22) | copy-start | bytes 1156
  56.6 0.8 copy-start.21
  57.1 0.8 copy-start.23
  57.1 0.9 copy-start.22
  67.1 14.9 %collective-permute-start.11 = (bf16[96,256]{1,0:T(8,128)(2,1)}, bf16[96,256]{1,0:T(8,128)(2,1)S(1)}, u32[]{:S(2)}, u32[]{:S(2)}) collective-permute-start(bf16[96,256]{1,0:T(8,128)(2,1)} %get-tuple-element.36), channel_id=1, source_target_pairs={{0,0},{16,32},{32,64},{48,96},{64,16},{80,48},{96,80},{112,112},{1... | collective-permute-start | bytes 147464 | tf_op jit(solution)/shard_map/ppermute | solution.py:29
  69.9 12.0 %collective-permute-start.12 = (bf16[96,256]{1,0:T(8,128)(2,1)}, bf16[96,256]{1,0:T(8,128)(2,1)S(1)}, u32[]{:S(2)}, u32[]{:S(2)}) collective-permute-start(bf16[96,256]{1,0:T(8,128)(2,1)} %get-tuple-element.37), channel_id=1, source_target_pairs={{0,64},{16,96},{32,0},{48,32},{64,80},{80,112},{96,16},{112,48},{1... | collective-permute-start | bytes 147464 | tf_op jit(solution)/shard_map/ppermute | solution.py:29
  71.0 12.6 %collective-permute-start.13 = (bf16[96,256]{1,0:T(8,128)(2,1)}, bf16[96,256]{1,0:T(8,128)(2,1)S(1)}, u32[]{:S(2)}, u32[]{:S(2)}) collective-permute-start(bf16[96,256]{1,0:T(8,128)(2,1)} %get-tuple-element.38), channel_id=1, source_target_pairs={{0,128},{16,160},{32,192},{48,224},{64,144},{80,176},{96,208},{112... | collective-permute-start | bytes 147464 | tf_op jit(solution)/shard_map/ppermute | solution.py:29
  79.1 6.7 %collective-permute-start.14 = (bf16[96,256]{1,0:T(8,128)(2,1)}, bf16[96,256]{1,0:T(8,128)(2,1)S(1)}, u32[]{:S(2)}, u32[]{:S(2)}) collective-permute-start(bf16[96,256]{1,0:T(8,128)(2,1)} %get-tuple-element.39), channel_id=1, source_target_pairs={{0,192},{16,224},{32,128},{48,160},{64,208},{80,240},{96,144},{112... | collective-permute-start | bytes 147464 | tf_op jit(solution)/shard_map/ppermute | solution.py:29
  82.0 3.8 %copy-start.8 = (bf16[96,256]{1,0:T(8,128)(2,1)}, bf16[96,256]{1,0:T(8,128)(2,1)S(1)}, u32[]{:S(2)}) copy-start(bf16[96,256]{1,0:T(8,128)(2,1)S(1)} %collective-permute-done.11.piece0) | copy-start | bytes 147460
  82.0 3.8 %copy-start.9 = (bf16[96,256]{1,0:T(8,128)(2,1)}, bf16[96,256]{1,0:T(8,128)(2,1)S(1)}, u32[]{:S(2)}) copy-start(bf16[96,256]{1,0:T(8,128)(2,1)S(1)} %collective-permute-done.12.piece1) | copy-start | bytes 147460
  83.6 2.2 %copy-start.10 = (bf16[96,256]{1,0:T(8,128)(2,1)}, bf16[96,256]{1,0:T(8,128)(2,1)S(1)}, u32[]{:S(2)}) copy-start(bf16[96,256]{1,0:T(8,128)(2,1)S(1)} %collective-permute-done.13.piece2) | copy-start | bytes 147460
  85.8 0.6 copy-start.11
  88.1 31.0 %collective-permute-start.20 = (bf16[96,2048]{1,0:T(8,128)(2,1)}, bf16[96,2048]{1,0:T(8,128)(2,1)S(1)}, u32[]{:S(2)}, u32[]{:S(2)}) collective-permute-start(bf16[96,2048]{1,0:T(8,128)(2,1)} %collective-permute-done.4.near0), channel_id=1, source_target_pairs={{0,64},{64,0},{1,65},{65,1},{2,66},{66,2},{3,67},{67,3},{4,68},{68... | collective-permute-start | bytes 1179656 | tf_op jit(solution)/shard_map/ppermute | solution.py:29
  89.6 29.5 %collective-permute-start.21 = (bf16[96,2048]{1,0:T(8,128)(2,1)}, bf16[96,2048]{1,0:T(8,128)(2,1)S(1)}, u32[]{:S(2)}, u32[]{:S(2)}) collective-permute-start(bf16[96,2048]{1,0:T(8,128)(2,1)} %collective-permute-done.5.near1), channel_id=1, source_target_pairs={{0,64},{64,0},{1,65},{65,1},{2,66},{66,2},{3,67},{67,3},{4,68},{68... | collective-permute-start | bytes 1179656 | tf_op jit(solution)/shard_map/ppermute | solution.py:29
  89.7 10.4 %collective-permute-start.18 = (bf16[96,512]{1,0:T(8,128)(2,1)}, bf16[96,512]{1,0:T(8,128)(2,1)S(1)}, u32[]{:S(2)}, u32[]{:S(2)}) collective-permute-start(bf16[96,512]{1,0:T(8,128)(2,1)} %get-tuple-element.42), channel_id=1, source_target_pairs={{0,4},{4,8},{8,12},{12,16},{16,20},{20,24},{24,28},{28,32},{32,36}... | collective-permute-start | bytes 294920 | tf_op jit(solution)/shard_map/ppermute | solution.py:29
  93.3 8.1 %collective-permute-start.19 = (bf16[96,512]{1,0:T(8,128)(2,1)}, bf16[96,512]{1,0:T(8,128)(2,1)S(1)}, u32[]{:S(2)}, u32[]{:S(2)}) collective-permute-start(bf16[96,512]{1,0:T(8,128)(2,1)} %get-tuple-element.43), channel_id=1, source_target_pairs={{4,0},{8,4},{12,8},{16,12},{20,16},{24,20},{28,24},{32,28},{36,32}... | collective-permute-start | bytes 294920 | tf_op jit(solution)/shard_map/ppermute | solution.py:29
  98.5 14.1 %collective-permute-start.17 = (bf16[96,1024]{1,0:T(8,128)(2,1)}, bf16[96,1024]{1,0:T(8,128)(2,1)S(1)}, u32[]{:S(2)}, u32[]{:S(2)}) collective-permute-start(bf16[96,1024]{1,0:T(8,128)(2,1)} %get-tuple-element.44.clip0.clip), channel_id=1, source_target_pairs={{0,3},{1,0},{2,1},{3,2},{4,7},{5,4},{6,5},{7,6},{8,11},{9,8},{10,9... | collective-permute-start | bytes 589832 | tf_op jit(solution)/shard_map/ppermute | solution.py:29
  100.1 19.1 %copy-start.29 = (bf16[96,512]{1,0:T(8,128)(2,1)}, bf16[96,512]{1,0:T(8,128)(2,1)S(1)}, u32[]{:S(2)}) copy-start(bf16[96,512]{1,0:T(8,128)(2,1)S(1)} %collective-permute-done.18.before) | copy-start | bytes 294916
  100.1 12.6 %collective-permute-start.16 = (bf16[96,1024]{1,0:T(8,128)(2,1)}, bf16[96,1024]{1,0:T(8,128)(2,1)S(1)}, u32[]{:S(2)}, u32[]{:S(2)}) collective-permute-start(bf16[96,1024]{1,0:T(8,128)(2,1)} %get-tuple-element.44.clip0.clip), channel_id=1, source_target_pairs={{0,2},{1,3},{2,0},{3,1},{4,6},{5,7},{6,4},{7,5},{8,10},{9,11},{10,... | collective-permute-start | bytes 589832 | tf_op jit(solution)/shard_map/ppermute | solution.py:29
  101.4 17.8 %copy-start.30 = (bf16[96,512]{1,0:T(8,128)(2,1)}, bf16[96,512]{1,0:T(8,128)(2,1)S(1)}, u32[]{:S(2)}) copy-start(bf16[96,512]{1,0:T(8,128)(2,1)S(1)} %collective-permute-done.19.after) | copy-start | bytes 294916
  101.4 11.5 %collective-permute-start.15 = (bf16[96,1024]{1,0:T(8,128)(2,1)}, bf16[96,1024]{1,0:T(8,128)(2,1)S(1)}, u32[]{:S(2)}, u32[]{:S(2)}) collective-permute-start(bf16[96,1024]{1,0:T(8,128)(2,1)} %get-tuple-element.44.clip0.clip), channel_id=1, source_target_pairs={{0,1},{1,2},{2,3},{3,0},{4,5},{5,6},{6,7},{7,4},{8,9},{9,10},{10,1... | collective-permute-start | bytes 589832 | tf_op jit(solution)/shard_map/ppermute | solution.py:29
  102.8 16.3 %all-to-all-start.1 = ((f32[64,1,128]{2,1,0:T(1,128)}), f32[64,1,128]{2,1,0:T(1,128)S(1)}, u32[]{:S(2)}, u32[]{:S(2)}) async-start(f32[64,1,128]{2,1,0:T(1,128)} %get-tuple-element.41), calls=%async_computation.1 | async-start | bytes 65536 | tf_op jit(solution)/shard_map/all_to_all | solution.py:450
  112.7 6.5 %copy-start.26 = (bf16[96,1024]{1,0:T(8,128)(2,1)}, bf16[96,1024]{1,0:T(8,128)(2,1)S(1)}, u32[]{:S(2)}) copy-start(bf16[96,1024]{1,0:T(8,128)(2,1)S(1)} %collective-permute-done.17.clip3) | copy-start | bytes 589828
  112.7 6.5 %copy-start.27 = (bf16[96,1024]{1,0:T(8,128)(2,1)}, bf16[96,1024]{1,0:T(8,128)(2,1)S(1)}, u32[]{:S(2)}) copy-start(bf16[96,1024]{1,0:T(8,128)(2,1)S(1)} %collective-permute-done.16.clip2) | copy-start | bytes 589828
  112.8 6.4 %copy-start.28 = (bf16[96,1024]{1,0:T(8,128)(2,1)}, bf16[96,1024]{1,0:T(8,128)(2,1)S(1)}, u32[]{:S(2)}) copy-start(bf16[96,1024]{1,0:T(8,128)(2,1)S(1)} %collective-permute-done.15.clip1) | copy-start | bytes 589828
  119.1 0.6 copy-start.12
  119.1 0.8 copy-start.24
  119.2 0.9 copy-start.25
  120.0 12.2 %copy-start.1 = (bf16[3,3,3,96,384]{4,3,2,1,0:T(8,128)(2,1)S(1)}, bf16[3,3,3,96,384]{4,3,2,1,0:T(8,128)(2,1)}, u32[]{:S(2)}) copy-start(bf16[3,3,3,96,384]{4,3,2,1,0:T(8,128)(2,1)} %param.23) | copy-start | bytes 5971972
  126.5 20.6 %all-to-all-start.2 = ((bf16[16,8,16,128]{3,2,1,0:T(8,128)(2,1)}), bf16[16,8,16,128]{3,2,1,0:T(8,128)(2,1)S(1)}, u32[]{:S(2)}, u32[]{:S(2)}) async-start(bf16[16,8,16,128]{3,2,1,0:T(8,128)(2,1)} %bitcast.48), calls=%async_computation.2 | async-start | bytes 1048576 | tf_op jit(solution)/shard_map/all_to_all | solution.py:474
  140.5 5.5 %collective-permute-start.22 = (bf16[2,96,1024]{2,1,0:T(8,128)(2,1)}, bf16[2,96,1024]{2,1,0:T(8,128)(2,1)S(1)}, u32[]{:S(2)}, u32[]{:S(2)}) collective-permute-start(bf16[2,96,1024]{2,1,0:T(8,128)(2,1)} %get-tuple-element.57), channel_id=1, source_target_pairs={{0,64},{64,0},{1,65},{65,1},{2,66},{66,2},{3,67},{67,3},{4,68},{68... | collective-permute-start | bytes 1179656 | tf_op jit(solution)/shard_map/ppermute | solution.py:29
  147.0 35.9 %copy-start.7 = (bf16[96,1024]{1,0:T(8,128)(2,1)S(1)}, bf16[96,1024]{1,0:T(8,128)(2,1)}, u32[]{:S(2)}) copy-start(bf16[96,1024]{1,0:T(8,128)(2,1)} %get-tuple-element.44.clip0.clip) | copy-start | bytes 589828
  147.0 35.9 %copy-start.17 = (f32[96]{0:T(128)S(1)}, f32[96]{0:T(128)}, u32[]{:S(2)}) copy-start(f32[96]{0:T(128)} %param.24) | copy-start | bytes 1156
  168.7 28.6 %copy-start = (bf16[16,8,16,128]{3,2,1,0:T(8,128)(2,1)}, bf16[16,8,16,128]{3,2,1,0:T(8,128)(2,1)S(1)}, u32[]{:S(2)}) copy-start(bf16[16,8,16,128]{3,2,1,0:T(8,128)(2,1)S(1)} %all_to_all.20) | copy-start | bytes 1572868
  168.7 14.2 %collective-permute-start.23 = (bf16[96,1024]{1,0:T(8,128)(2,1)S(1)}, bf16[96,1024]{1,0:T(8,128)(2,1)S(1)}, u32[]{:S(2)}, u32[]{:S(2)}) collective-permute-start(bf16[96,1024]{1,0:T(8,128)(2,1)S(1)} %fusion.1), channel_id=1, source_target_pairs={{0,128},{128,0},{1,129},{129,1},{2,130},{130,2},{3,131},{131,3},{4... | collective-permute-start | bytes 589832 | tf_op jit(solution)/shard_map/ppermute | solution.py:29
  170.2 14.1 %collective-permute-start.26 = (bf16[128,16,128]{2,1,0:T(8,128)(2,1)S(1)}, bf16[128,16,128]{2,1,0:T(8,128)(2,1)S(1)}, u32[]{:S(2)}, u32[]{:S(2)}) collective-permute-start(bf16[128,16,128]{2,1,0:T(8,128)(2,1)S(1)} %bitcast.43), channel_id=1, source_target_pairs={{0,3},{1,0},{2,1},{3,2},{4,7},{5,4},{6,5},{7,6},{8,11},{9,8},{10,9... | collective-permute-start | bytes 1572872 | tf_op jit(solution)/shard_map/ppermute | solution.py:29
  170.8 13.5 %collective-permute-start.25 = (bf16[128,16,128]{2,1,0:T(8,128)(2,1)S(1)}, bf16[128,16,128]{2,1,0:T(8,128)(2,1)S(1)}, u32[]{:S(2)}, u32[]{:S(2)}) collective-permute-start(bf16[128,16,128]{2,1,0:T(8,128)(2,1)S(1)} %bitcast.44), channel_id=1, source_target_pairs={{0,2},{1,3},{2,0},{3,1},{4,6},{5,7},{6,4},{7,5},{8,10},{9,11},{10,... | collective-permute-start | bytes 1572872 | tf_op jit(solution)/shard_map/ppermute | solution.py:29
  172.2 25.1 %collective-permute-start.24 = (bf16[128,16,128]{2,1,0:T(8,128)(2,1)S(1)}, bf16[128,16,128]{2,1,0:T(8,128)(2,1)S(1)}, u32[]{:S(2)}, u32[]{:S(2)}) collective-permute-start(bf16[128,16,128]{2,1,0:T(8,128)(2,1)S(1)} %bitcast.45), channel_id=1, source_target_pairs={{0,1},{1,2},{2,3},{3,0},{4,5},{5,6},{6,7},{7,4},{8,9},{9,10},{10,1... | collective-permute-start | bytes 1572872 | tf_op jit(solution)/shard_map/ppermute | solution.py:29
  184.3 13.1 %copy-start.3 = (bf16[128,16,128]{2,1,0:T(8,128)(2,1)}, bf16[128,16,128]{2,1,0:T(8,128)(2,1)S(1)}, u32[]{:S(2)}) copy-start(bf16[128,16,128]{2,1,0:T(8,128)(2,1)S(1)} %collective-permute-done.26.table3) | copy-start | bytes 1572868
  184.3 13.1 %copy-start.4 = (bf16[128,16,128]{2,1,0:T(8,128)(2,1)}, bf16[128,16,128]{2,1,0:T(8,128)(2,1)S(1)}, u32[]{:S(2)}) copy-start(bf16[128,16,128]{2,1,0:T(8,128)(2,1)S(1)} %collective-permute-done.25.table2) | copy-start | bytes 1572868
  197.4 0.8 copy-start.5
